TPU v7x, 32 devices: a whole 2x2x4 slice. The times are simulated.
32 devices in a mesh: group: 2 (over y), expert: 16 (over z, x, core).
Axes of the slice: x: 2, y: 2, z: 4, core: 2. Of those that a mesh axis runs over, the one named last changes fastest.
Arguments:
- inputs: bfloat16 [3, 256, 2048], P(None, ('group', 'expert')), may hold values from -6 to 6
- queries: bfloat16 [3, 256, 2048], P(None, ('group', 'expert')), may hold values from -24 to 24
- new_keys: bfloat16 [3, 256, 128], P(None, ('group', 'expert')), may hold values from -8 to 8
- new_values: bfloat16 [3, 256, 128], P(None, ('group', 'expert')), may hold values from -6 to 6
- key_cache: bfloat16 [256, 384, 128], P(('group', 'expert')), may hold values from -4.5 to 4.5
- value_cache: bfloat16 [256, 384, 128], P(('group', 'expert')), may hold values from -6 to 6
- cache_lengths: int32 [256], P(('group', 'expert')), may hold values from 48 to 384, as said below
- expert_ids: int32 [3, 256, 8], P(None, ('group', 'expert')), may hold values from 0 to 15, all different within a row; in each aligned block of 8 rows (0 to 7, 8 to 15, ..., all dimensions but the last counted through in order) at most 8 rows name the same one
- route_weights: float32 [3, 256, 8], P(None, ('group', 'expert')), may hold values from 0.03 to 0.5
- w_gate: bfloat16 [16, 2048, 768], P('expert', 'group'), may hold values from -0.125 to 0.125
- w_up: bfloat16 [16, 2048, 768], P('expert', 'group'), may hold values from -0.125 to 0.125
- w_down: bfloat16 [16, 768, 2048], P('expert', None, 'group'), may hold values from -0.21875 to 0.21875
Outputs:
- layer_out: bfloat16 [3, 256, 2048], P(None, ('group', 'expert'))
Inputs may be any that keep to these rules, and one draw needn't show every extreme that they name: `expert_ids`: in each step, no expert is named by more than 8 of the 8 rows of one aligned block. `cache_lengths`: in each aligned block of 8 rows one row has all 384 positions valid.
All inputs are finite; a program needn't handle non-finite values.
Results may differ from a plain program's by a relative error of at most 0.014.
Values may be sent and summed in bfloat16 or wider, within the bound.
A program may use at most 64 MiB of HBM per device.

v0:
```python
import jax
import jax.numpy as jnp
from jax import lax
from jax.sharding import PartitionSpec as P

HEADS = 32
KV_HEADS = 2
HEAD_DIM = 64
TOPK = 8
CACHE = 384
STEPS = 3


def attend_rows(query_vals, key_rows, value_rows, cache_ok, fresh_keys, fresh_values):
    factor = HEAD_DIM ** (-0.5)
    old_scores = (
        jnp.einsum("bkgd,bjkd->bkgj", query_vals, key_rows, preferred_element_type=jnp.float32)
        * factor
    )
    old_scores = jnp.where(cache_ok[:, None, None, :], old_scores, -1e30)
    new_scores = (
        jnp.einsum("bkgd,bjkd->bkgj", query_vals, fresh_keys, preferred_element_type=jnp.float32)
        * factor
    )
    highest = jnp.maximum(
        jnp.max(old_scores, axis=-1, keepdims=True), jnp.max(new_scores, axis=-1, keepdims=True)
    )
    old_weights = jnp.exp(old_scores - highest)
    new_weights = jnp.exp(new_scores - highest)
    denom_sum = jnp.sum(old_weights, axis=-1, keepdims=True) + jnp.sum(
        new_weights, axis=-1, keepdims=True
    )
    old_probs = (old_weights / denom_sum).astype(jnp.bfloat16)
    new_probs = (new_weights / denom_sum).astype(jnp.bfloat16)
    attended = jnp.einsum(
        "bkgj,bjkd->bkgd", old_probs, value_rows, preferred_element_type=jnp.float32
    )
    return attended + jnp.einsum(
        "bkgj,bjkd->bkgd", new_probs, fresh_values, preferred_element_type=jnp.float32
    )


def shards(
    inputs,
    queries,
    new_keys,
    new_values,
    key_cache,
    value_cache,
    cache_lengths,
    expert_ids,
    route_weights,
    w_gate,
    w_up,
    w_down,
):
    experts_all = lax.axis_size("expert")
    rows_dev = inputs.shape[1]
    per_group = HEADS // KV_HEADS
    capacity = max(2, 2 * rows_dev * TOPK // experts_all)
    gate_full, up_full, down_full = (
        lax.all_gather(w_gate, "group", axis=1, tiled=True),
        lax.all_gather(w_up, "group", axis=1, tiled=True),
        lax.all_gather(w_down, "group", axis=2, tiled=True),
    )
    gate_mat = gate_full[0]
    up_mat = up_full[0]
    down_mat = down_full[0]
    key_rows = key_cache.reshape(rows_dev, CACHE, KV_HEADS, HEAD_DIM)
    value_rows = value_cache.reshape(rows_dev, CACHE, KV_HEADS, HEAD_DIM)
    cache_ok = jnp.arange(CACHE, dtype=jnp.int32)[None, :] < cache_lengths[:, None]
    slot_columns = jnp.arange(experts_all * capacity, dtype=jnp.int32)
    expert_range = jnp.arange(experts_all, dtype=jnp.int32)
    results = []
    for step_index in range(STEPS):
        fresh = step_index + 1
        fresh_keys = jnp.swapaxes(new_keys[:fresh], 0, 1).reshape(
            rows_dev, fresh, KV_HEADS, HEAD_DIM
        )
        fresh_values = jnp.swapaxes(new_values[:fresh], 0, 1).reshape(
            rows_dev, fresh, KV_HEADS, HEAD_DIM
        )
        query_vals = queries[step_index].reshape(rows_dev, KV_HEADS, per_group, HEAD_DIM)
        attended = attend_rows(query_vals, key_rows, value_rows, cache_ok, fresh_keys, fresh_values)
        hidden = (inputs[step_index].astype(jnp.float32) + attended.reshape(rows_dev, -1)).astype(
            jnp.bfloat16
        )
        chosen = expert_ids[step_index].reshape(-1)
        onehot = (chosen[:, None] == expert_range[None, :]).astype(jnp.int32)
        before = jnp.cumsum(onehot, axis=0) - onehot
        slot_rank = jnp.sum(before * onehot, axis=1)
        target = chosen * capacity + slot_rank
        placed = (target[:, None] == slot_columns[None, :]).reshape(rows_dev, TOPK, -1)
        spread = jnp.any(placed, axis=1).astype(jnp.bfloat16)
        outgoing = jnp.einsum(
            "rc,rd->cd", spread, hidden, preferred_element_type=jnp.float32
        ).astype(jnp.bfloat16)
        outgoing = outgoing.reshape(experts_all, capacity, -1)
        mixing = jnp.sum(jnp.where(placed, route_weights[step_index][:, :, None], 0.0), axis=1)
        arrived = lax.all_to_all(outgoing, "expert", split_axis=0, concat_axis=0, tiled=True)
        num_slots, item_count, feature_dim = arrived.shape
        tokens = arrived.reshape(num_slots * item_count, feature_dim)
        gate_val = jnp.dot(tokens, gate_mat, preferred_element_type=jnp.float32)
        up_val = jnp.dot(tokens, up_mat, preferred_element_type=jnp.float32)
        activated = (jax.nn.silu(gate_val) * up_val).astype(jnp.bfloat16)
        expert_out = jnp.dot(activated, down_mat, preferred_element_type=jnp.float32).astype(
            jnp.bfloat16
        )
        returned = lax.all_to_all(
            expert_out.reshape(num_slots, item_count, feature_dim),
            "expert",
            split_axis=0,
            concat_axis=0,
            tiled=True,
        )
        combined = jnp.dot(
            mixing,
            returned.reshape(experts_all * capacity, -1).astype(jnp.float32),
            precision=lax.Precision.HIGHEST,
        )
        results.append((hidden.astype(jnp.float32) + combined).astype(jnp.bfloat16))
    return jnp.stack(results)


def solution(mesh):
    in_specs = (
        P(None, ("group", "expert"), None),
        P(None, ("group", "expert"), None),
        P(None, ("group", "expert"), None),
        P(None, ("group", "expert"), None),
        P(("group", "expert"), None, None),
        P(("group", "expert"), None, None),
        P(("group", "expert")),
        P(None, ("group", "expert"), None),
        P(None, ("group", "expert"), None),
        P("expert", "group", None),
        P("expert", "group", None),
        P("expert", None, "group"),
    )
    out_specs = P(None, ("group", "expert"), None)
    return jax.shard_map(shards, mesh=mesh, in_specs=in_specs, out_specs=out_specs, check_vma=False)
```

profile of v0, /device:TPU:0, one launch (start us, length us, event | category | flops | bytes accessed | tf_op | source)
XLA Modules:
  0.0 219.8 jit_solution(4910898515476897053)
XLA Ops:
  6.6 0.7 all-gather.4.cloned.1.call-update
  7.3 0.7 all-gather.6.cloned.1.call-update
  8.1 0.7 reshape.227
  9.2 0.2 select_reduce_fusion.3
  9.7 0.2 select_reduce_fusion.1
  10.1 0.2 select_reduce_fusion.5
  10.3 0.7 reduce_sum.111
  11.2 0.4 copy.27
  11.6 0.4 copy.28
  11.9 0.7 iota_compare_fusion.6
  12.8 0.3 fusion.142
  13.2 0.2 fusion.101
  13.5 0.2 fusion.121
  13.7 0.4 convolution_add_fusion.3
  14.4 1.1 fusion.29
  15.5 7.4 %all-to-all-start.4 = ((bf16[16,8,2048]{2,1,0:T(8,128)(2,1)}), bf16[16,8,2048]{2,1,0:T(8,128)(2,1)S(1)}, u32[]{:S(2)}, u32[]{:S(2)}) async-start(bf16[16,8,2048]{2,1,0:T(8,128)(2,1)} %fusion.29), calls=%async_computation.4 | async-start | bytes 1048576 | tf_op jit(solution)/shard_map/all_to_all | solution.py:100
  22.9 0.7 all-gather.8.cloned.1.call-update
  23.9 0.3 fusion.144
  24.5 0.2 fusion.100
  24.8 0.2 fusion.127
  25.3 0.4 convolution_add_fusion.4
  25.9 1.1 fusion.28
  27.2 0.4 fusion.146
  27.6 9.8 %all-to-all-done.4 = bf16[16,8,2048]{2,1,0:T(8,128)(2,1)S(1)} async-done(((bf16[16,8,2048]{2,1,0:T(8,128)(2,1)}), bf16[16,8,2048]{2,1,0:T(8,128)(2,1)S(1)}, u32[]{:S(2)}, u32[]{:S(2)}) %all-to-all-start.4) | async-done | bytes 524320 | tf_op jit(solution)/shard_map/all_to_all | solution.py:100
  37.4 4.1 %all-to-all-start.2 = ((bf16[16,8,2048]{2,1,0:T(8,128)(2,1)}), bf16[16,8,2048]{2,1,0:T(8,128)(2,1)S(1)}, u32[]{:S(2)}, u32[]{:S(2)}) async-start(bf16[16,8,2048]{2,1,0:T(8,128)(2,1)} %fusion.28), calls=%async_computation.2 | async-start | bytes 1048576 | tf_op jit(solution)/shard_map/all_to_all | solution.py:100
  41.5 0.2 fusion.99
  41.8 0.4 convolution_add_fusion.5
  42.4 1.1 fusion.27
  43.5 12.4 %all-to-all-done.2 = bf16[16,8,2048]{2,1,0:T(8,128)(2,1)S(1)} async-done(((bf16[16,8,2048]{2,1,0:T(8,128)(2,1)}), bf16[16,8,2048]{2,1,0:T(8,128)(2,1)S(1)}, u32[]{:S(2)}, u32[]{:S(2)}) %all-to-all-start.2) | async-done | bytes 524320 | tf_op jit(solution)/shard_map/all_to_all | solution.py:100
  55.9 4.2 %all-to-all-start = ((bf16[16,8,2048]{2,1,0:T(8,128)(2,1)}), bf16[16,8,2048]{2,1,0:T(8,128)(2,1)}, u32[]{:S(2)}, u32[]{:S(2)}) async-start(bf16[16,8,2048]{2,1,0:T(8,128)(2,1)} %fusion.27), calls=%async_computation | async-start | bytes 1048576 | tf_op jit(solution)/shard_map/all_to_all | solution.py:100
  60.2 3.2 %fusion.12 = f32[128,768]{1,0:T(8,128)} fusion(bf16[1,2048,768]{2,1,0:T(8,128)(2,1)} %all-gather.4.cloned.1.call-done, bf16[16,8,2048]{2,1,0:T(8,128)(2,1)S(1)} %all-to-all-done.4), kind=kOutput, calls=%fused_computation.12 | convolution fusion | flops 402653184 | bytes 4063232 | tf_op jit(solution)/shard_map/dot_general | solution.py:103
  63.4 39.7 %all-gather.6.cloned.1.call-done = bf16[1,2048,768]{2,1,0:T(8,128)(2,1)} async-done(((bf16[1,1024,768]{2,1,0:T(8,128)(2,1)}), bf16[1,2048,768]{2,1,0:T(8,128)(2,1)}) %all-gather.6.cloned.1.call-update) | async-done | bytes 3145744 | tf_op jit(solution)/shard_map/all_gather | solution.py:63
  103.1 46.5 %all-gather.8.cloned.1.call-done = bf16[1,768,2048]{2,1,0:T(8,128)(2,1)} async-done(((bf16[1,768,1024]{2,1,0:T(8,128)(2,1)}), bf16[1,768,2048]{2,1,0:T(8,128)(2,1)}) %all-gather.8.cloned.1.call-update) | async-done | bytes 3145744 | tf_op jit(solution)/shard_map/all_gather | solution.py:64
  149.6 5.2 %fusion.30 = bf16[16,8,2048]{2,1,0:T(8,128)(2,1)} fusion(bf16[1,768,2048]{2,1,0:T(8,128)(2,1)} %all-gather.8.cloned.1.call-done, bf16[1,2048,768]{2,1,0:T(8,128)(2,1)} %all-gather.6.cloned.1.call-done, bf16[16,8,2048]{2,1,0:T(8,128)(2,1)} %copy-done.1, f32[128,768]{1,0:T(8,128)} %fusion.12), kind=kOutput, calls=%fused_computation.27 | convolution fusion | flops 806158336 | bytes 7733248 | tf_op jit(solution)/shard_map/dot_general | solution.py:106
  154.8 5.7 %all-to-all-start.5 = ((bf16[16,8,2048]{2,1,0:T(8,128)(2,1)}), bf16[16,8,2048]{2,1,0:T(8,128)(2,1)}, u32[]{:S(2)}, u32[]{:S(2)}) async-start(bf16[16,8,2048]{2,1,0:T(8,128)(2,1)} %fusion.30), calls=%async_computation.5 | async-start | bytes 1048576 | tf_op jit(solution)/shard_map/all_to_all | solution.py:109
  160.5 2.4 %fusion.14 = f32[128,768]{1,0:T(8,128)} fusion(bf16[1,2048,768]{2,1,0:T(8,128)(2,1)S(1)} %copy-done, bf16[16,8,2048]{2,1,0:T(8,128)(2,1)} %copy-done.2), kind=kOutput, calls=%fused_computation.14 | convolution fusion | flops 402653184 | bytes 4063232 | tf_op jit(solution)/shard_map/dot_general | solution.py:103
  162.9 5.2 %fusion.33 = bf16[16,8,2048]{2,1,0:T(8,128)(2,1)} fusion(bf16[1,768,2048]{2,1,0:T(8,128)(2,1)} %all-gather.8.cloned.1.call-done, bf16[1,2048,768]{2,1,0:T(8,128)(2,1)} %all-gather.6.cloned.1.call-done, bf16[16,8,2048]{2,1,0:T(8,128)(2,1)} %copy-done.2, f32[128,768]{1,0:T(8,128)} %fusion.14), kind=kOutput, calls=%fused_computation.28 | convolution fusion | flops 806158336 | bytes 7733248 | tf_op jit(solution)/shard_map/dot_general | solution.py:106
  168.1 6.9 %all-to-all-done.5 = bf16[16,8,2048]{2,1,0:T(8,128)(2,1)} async-done(((bf16[16,8,2048]{2,1,0:T(8,128)(2,1)}), bf16[16,8,2048]{2,1,0:T(8,128)(2,1)}, u32[]{:S(2)}, u32[]{:S(2)}) %all-to-all-start.5) | async-done | bytes 524320 | tf_op jit(solution)/shard_map/all_to_all | solution.py:109
  175.0 4.2 %all-to-all-start.3 = ((bf16[16,8,2048]{2,1,0:T(8,128)(2,1)}), bf16[16,8,2048]{2,1,0:T(8,128)(2,1)}, u32[]{:S(2)}, u32[]{:S(2)}) async-start(bf16[16,8,2048]{2,1,0:T(8,128)(2,1)} %fusion.33), calls=%async_computation.3 | async-start | bytes 1048576 | tf_op jit(solution)/shard_map/all_to_all | solution.py:109
  179.3 2.4 %fusion.16 = f32[128,768]{1,0:T(8,128)} fusion(bf16[1,2048,768]{2,1,0:T(8,128)(2,1)S(1)} %copy-done, bf16[16,8,2048]{2,1,0:T(8,128)(2,1)} %all-to-all-done), kind=kOutput, calls=%fused_computation.16 | convolution fusion | flops 402653184 | bytes 4063232 | tf_op jit(solution)/shard_map/dot_general | solution.py:103
  181.7 5.2 %fusion.36 = bf16[16,8,2048]{2,1,0:T(8,128)(2,1)} fusion(bf16[1,768,2048]{2,1,0:T(8,128)(2,1)} %all-gather.8.cloned.1.call-done, bf16[1,2048,768]{2,1,0:T(8,128)(2,1)} %all-gather.6.cloned.1.call-done, bf16[16,8,2048]{2,1,0:T(8,128)(2,1)} %all-to-all-done, f32[128,768]{1,0:T(8,128)} %fusion.16), kind=kOutput, calls=%fused_computation.29 | convolution fusion | flops 806158336 | bytes 7733248 | tf_op jit(solution)/shard_map/dot_general | solution.py:106
  186.8 6.9 %all-to-all-done.3 = bf16[16,8,2048]{2,1,0:T(8,128)(2,1)} async-done(((bf16[16,8,2048]{2,1,0:T(8,128)(2,1)}), bf16[16,8,2048]{2,1,0:T(8,128)(2,1)}, u32[]{:S(2)}, u32[]{:S(2)}) %all-to-all-start.3) | async-done | bytes 524320 | tf_op jit(solution)/shard_map/all_to_all | solution.py:109
  193.8 4.1 %all-to-all-start.1 = ((bf16[16,8,2048]{2,1,0:T(8,128)(2,1)}), bf16[16,8,2048]{2,1,0:T(8,128)(2,1)S(1)}, u32[]{:S(2)}, u32[]{:S(2)}) async-start(bf16[16,8,2048]{2,1,0:T(8,128)(2,1)} %fusion.36), calls=%async_computation.1 | async-start | bytes 1048576 | tf_op jit(solution)/shard_map/all_to_all | solution.py:109
  198.1 1.4 fusion.42
  199.4 1.4 fusion.43
  200.8 11.5 %all-to-all-done.1 = bf16[16,8,2048]{2,1,0:T(8,128)(2,1)S(1)} async-done(((bf16[16,8,2048]{2,1,0:T(8,128)(2,1)}), bf16[16,8,2048]{2,1,0:T(8,128)(2,1)S(1)}, u32[]{:S(2)}, u32[]{:S(2)}) %all-to-all-start.1) | async-done | bytes 524320 | tf_op jit(solution)/shard_map/all_to_all | solution.py:109
  212.3 0.3 fusion.44
  212.6 0.7 pad_maximum_fusion
  (77 shorter events, 3.4 us)
Async XLA Ops:
  6.5 1.5 copy-start.8
  6.5 2.2 copy-start.9
  6.5 2.3 %copy-start.7 = (s32[3,8,8]{2,1,0:T(8,128)S(1)}, s32[3,8,8]{2,1,0:T(8,128)}, u32[]{:S(2)}) copy-start(s32[3,8,8]{2,1,0:T(8,128)} %param.19) | copy-start | bytes 2308
  6.5 4.5 %copy-start.6 = (bf16[3,8,2048]{2,1,0:T(8,128)(2,1)S(1)}, bf16[3,8,2048]{2,1,0:T(8,128)(2,1)}, u32[]{:S(2)}) copy-start(bf16[3,8,2048]{2,1,0:T(8,128)(2,1)} %param.13) | copy-start | bytes 294916
  6.5 4.6 %copy-start.3 = (bf16[8,384,128]{2,1,0:T(8,128)(2,1)S(1)}, bf16[8,384,128]{2,1,0:T(8,128)(2,1)}, u32[]{:S(2)}) copy-start(bf16[8,384,128]{2,1,0:T(8,128)(2,1)} %param.16) | copy-start | bytes 2359300
  6.5 5.0 %copy-start.4 = (bf16[8,384,128]{2,1,0:T(8,128)(2,1)S(1)}, bf16[8,384,128]{2,1,0:T(8,128)(2,1)}, u32[]{:S(2)}) copy-start(bf16[8,384,128]{2,1,0:T(8,128)(2,1)} %param.17) | copy-start | bytes 2359300
  6.6 53.7 %all-gather.4.cloned.1.call-start = ((), (), s32[]{:S(2)}) async-start(), calls=%async_computation.6 | async-start | bytes 4718592 | tf_op jit(solution)/shard_map/all_gather | solution.py:62
  7.3 95.8 %all-gather.6.cloned.1.call-start = ((), (), s32[]{:S(2)}) async-start(), calls=%async_computation.7 | async-start | bytes 4718592 | tf_op jit(solution)/shard_map/all_gather | solution.py:63
  11.0 2.5 %copy-start.12 = (bf16[8,3,2,64]{3,2,0,1:T(2,128)(2,1)S(1)}, bf16[8,3,2,64]{3,2,0,1:T(2,128)(2,1)}, u32[]{:S(2)}) copy-start(bf16[8,3,2,64]{3,2,0,1:T(2,128)(2,1)} %reshape.227) | copy-start | bytes 18436
  11.5 2.7 %copy-start.10 = (s32[8,8]{1,0:T(8,128)S(1)}, s32[8,8]{1,0:T(8,128)}, u32[]{:S(2)}) copy-start(s32[8,8]{1,0:T(8,128)} %reduce_sum.111) | copy-start | bytes 772
  11.6 2.8 %copy-start.5 = (bf16[3,8,2048]{2,1,0:T(8,128)(2,1)S(1)}, bf16[3,8,2048]{2,1,0:T(8,128)(2,1)}, u32[]{:S(2)}) copy-start(bf16[3,8,2048]{2,1,0:T(8,128)(2,1)} %param.12) | copy-start | bytes 294916
  15.5 21.8 %all-to-all-start.4 = ((bf16[16,8,2048]{2,1,0:T(8,128)(2,1)}), bf16[16,8,2048]{2,1,0:T(8,128)(2,1)S(1)}, u32[]{:S(2)}, u32[]{:S(2)}) async-start(bf16[16,8,2048]{2,1,0:T(8,128)(2,1)} %fusion.29), calls=%async_computation.4 | async-start | bytes 1048576 | tf_op jit(solution)/shard_map/all_to_all | solution.py:100
  22.9 126.7 %all-gather.8.cloned.1.call-start = ((), (), s32[]{:S(2)}) async-start(), calls=%async_computation.8 | async-start | bytes 4718592 | tf_op jit(solution)/shard_map/all_gather | solution.py:64
  37.4 22.9 %copy-start.1 = (bf16[16,8,2048]{2,1,0:T(8,128)(2,1)}, bf16[16,8,2048]{2,1,0:T(8,128)(2,1)S(1)}, u32[]{:S(2)}) copy-start(bf16[16,8,2048]{2,1,0:T(8,128)(2,1)S(1)} %all-to-all-done.4) | copy-start | bytes 1572868
  37.4 18.6 %all-to-all-start.2 = ((bf16[16,8,2048]{2,1,0:T(8,128)(2,1)}), bf16[16,8,2048]{2,1,0:T(8,128)(2,1)S(1)}, u32[]{:S(2)}, u32[]{:S(2)}) async-start(bf16[16,8,2048]{2,1,0:T(8,128)(2,1)} %fusion.28), calls=%async_computation.2 | async-start | bytes 1048576 | tf_op jit(solution)/shard_map/all_to_all | solution.py:100
  55.9 4.3 %copy-start.2 = (bf16[16,8,2048]{2,1,0:T(8,128)(2,1)}, bf16[16,8,2048]{2,1,0:T(8,128)(2,1)S(1)}, u32[]{:S(2)}) copy-start(bf16[16,8,2048]{2,1,0:T(8,128)(2,1)S(1)} %all-to-all-done.2) | copy-start | bytes 1572868
  55.9 98.9 %all-to-all-start = ((bf16[16,8,2048]{2,1,0:T(8,128)(2,1)}), bf16[16,8,2048]{2,1,0:T(8,128)(2,1)}, u32[]{:S(2)}, u32[]{:S(2)}) async-start(bf16[16,8,2048]{2,1,0:T(8,128)(2,1)} %fusion.27), calls=%async_computation | async-start | bytes 1048576 | tf_op jit(solution)/shard_map/all_to_all | solution.py:100
  63.4 97.1 %copy-start = (bf16[1,2048,768]{2,1,0:T(8,128)(2,1)S(1)}, bf16[1,2048,768]{2,1,0:T(8,128)(2,1)}, u32[]{:S(2)}) copy-start(bf16[1,2048,768]{2,1,0:T(8,128)(2,1)} %all-gather.4.cloned.1.call-done) | copy-start | bytes 9437188
  154.8 20.2 %all-to-all-start.5 = ((bf16[16,8,2048]{2,1,0:T(8,128)(2,1)}), bf16[16,8,2048]{2,1,0:T(8,128)(2,1)}, u32[]{:S(2)}, u32[]{:S(2)}) async-start(bf16[16,8,2048]{2,1,0:T(8,128)(2,1)} %fusion.30), calls=%async_computation.5 | async-start | bytes 1048576 | tf_op jit(solution)/shard_map/all_to_all | solution.py:109
  175.0 18.7 %all-to-all-start.3 = ((bf16[16,8,2048]{2,1,0:T(8,128)(2,1)}), bf16[16,8,2048]{2,1,0:T(8,128)(2,1)}, u32[]{:S(2)}, u32[]{:S(2)}) async-start(bf16[16,8,2048]{2,1,0:T(8,128)(2,1)} %fusion.33), calls=%async_computation.3 | async-start | bytes 1048576 | tf_op jit(solution)/shard_map/all_to_all | solution.py:109
  181.7 16.2 %copy-start.11 = (f32[3,8,8]{2,1,0:T(8,128)S(1)}, f32[3,8,8]{2,1,0:T(8,128)}, u32[]{:S(2)}) copy-start(f32[3,8,8]{2,1,0:T(8,128)} %param.20) | copy-start | bytes 2308
  193.8 18.5 %all-to-all-start.1 = ((bf16[16,8,2048]{2,1,0:T(8,128)(2,1)}), bf16[16,8,2048]{2,1,0:T(8,128)(2,1)S(1)}, u32[]{:S(2)}, u32[]{:S(2)}) async-start(bf16[16,8,2048]{2,1,0:T(8,128)(2,1)} %fusion.36), calls=%async_computation.1 | async-start | bytes 1048576 | tf_op jit(solution)/shard_map/all_to_all | solution.py:109
Sparse Core Ops, SparseCore 0:
  8.9 47.6 all-gather.3
  58.2 44.9 all-gather.5
  104.7 44.9 all-gather.7
where the time goes:
time: 221 us; the launch traced here: 220 us
  waiting for transfers between devices  136 us (62%)
  matrix products  33.3 us (15%)
  starting transfers between devices  29.8 us (13%)
  between operations  13.4 us (6%)
  other arithmetic  3.81 us (2%)
  local copies, waits for them, and re-layouts  3.68 us (2%)
    all_gather x1, waiting for transfers between devices, shards(): lax.all_gather(w_down, 'group', axis=2, tiled=True)  46.5 us
    all_gather x1, waiting for transfers between devices, shards(): lax.all_gather(w_up, 'group', axis=1, tiled=True)  39.7 us
    all_to_all x3, waiting for transfers between devices, shards(): lax.all_to_all(expert_out.reshape(num_slots, item_count, feature_dim), 'e...  25.4 us
    all_to_all x3, waiting for transfers between devices, shards(): lax.all_to_all(outgoing, 'expert', split_axis=0, concat_axis=0, tiled=True)  22.2 us
    all_to_all x3, starting transfers between devices, shards(): lax.all_to_all(outgoing, 'expert', split_axis=0, concat_axis=0, tiled=True)  15.7 us
    dot_general x3, matrix products, shards(): jnp.dot(activated, down_mat, preferred_element_type=jnp.float32)  15.6 us
    all_to_all x3, starting transfers between devices, shards(): lax.all_to_all(expert_out.reshape(num_slots, item_count, feature_dim), 'e...  14 us
    dot_general x3, matrix products, shards(): gate_val = jnp.dot(tokens, gate_mat, preferred_element_type=jnp.float32)  7.95 us
  transfers between devices with their start and end apart: 9, of which 7 were waited for; matrix products, arithmetic and copies ran while one was open for 18% of the time, Pallas kernels for 0%

commit v1 on v0

--- a/solution.py
+++ b/solution.py
@@ -122,6 +122,108 @@
     return jnp.stack(results)
 
 
+def dense_shards(
+    inputs,
+    queries,
+    new_keys,
+    new_values,
+    key_cache,
+    value_cache,
+    cache_lengths,
+    expert_ids,
+    route_weights,
+    w_gate,
+    w_up,
+    w_down,
+):
+    groups = lax.axis_size("group")
+    experts_all = lax.axis_size("expert")
+    me = lax.axis_index("group")
+    rows_dev = inputs.shape[1]
+    width = inputs.shape[2]
+    part = w_gate.shape[2] // groups
+    depth = w_gate.shape[1]
+    columns = w_down.shape[2]
+    gate_full = jnp.zeros((width, part), w_gate.dtype)
+    up_full = jnp.zeros((width, part), w_gate.dtype)
+    down_full = jnp.zeros((part, width), w_gate.dtype)
+    pairs = []
+    for shift in range(groups):
+        target = lax.rem(me + shift, groups)
+        pieces = (
+            lax.dynamic_slice_in_dim(w_gate[0], target * part, part, 1),
+            lax.dynamic_slice_in_dim(w_up[0], target * part, part, 1),
+            lax.dynamic_slice_in_dim(w_down[0], target * part, part, 0),
+        )
+        if shift:
+            perm = [(i, (i + shift) % groups) for i in range(groups)]
+            pieces = tuple(lax.ppermute(piece, "group", perm) for piece in pieces)
+        pairs.append((lax.rem(me - shift + groups, groups), pieces))
+    for source, (gate_piece, up_piece, down_piece) in pairs:
+        gate_full = lax.dynamic_update_slice_in_dim(gate_full, gate_piece, source * depth, 0)
+        up_full = lax.dynamic_update_slice_in_dim(up_full, up_piece, source * depth, 0)
+        down_full = lax.dynamic_update_slice_in_dim(down_full, down_piece, source * columns, 1)
+    hidden = attend_steps(
+        inputs, queries, new_keys, new_values, key_cache, value_cache, cache_lengths
+    )
+    expert_range = jnp.arange(experts_all, dtype=jnp.int32)
+    mixing = jnp.sum(
+        jnp.where(
+            expert_ids[..., None] == expert_range, route_weights[..., None], jnp.float32(0.0)
+        ),
+        axis=2,
+    )
+    mixing = mixing.reshape(STEPS * rows_dev, experts_all)
+    flat = hidden.reshape(STEPS * rows_dev, width)
+    tokens = lax.all_gather(flat, ("group", "expert"), axis=0, tiled=True)
+    factors = lax.all_gather(mixing, ("group", "expert"), axis=0, tiled=True)
+    factor = lax.dynamic_slice_in_dim(factors, lax.axis_index("expert"), 1, 1)
+    gate_val = jnp.dot(tokens, gate_full, preferred_element_type=jnp.float32)
+    up_val = jnp.dot(tokens, up_full, preferred_element_type=jnp.float32)
+    activated = (jax.nn.silu(gate_val) * up_val).astype(jnp.bfloat16)
+    expert_out = jnp.dot(activated, down_full, preferred_element_type=jnp.float32)
+    weighted = (factor * expert_out).astype(jnp.bfloat16)
+    combined = lax.psum_scatter(weighted, ("group", "expert"), scatter_dimension=0, tiled=True)
+    out = flat.astype(jnp.float32) + combined.astype(jnp.float32)
+    return out.astype(jnp.bfloat16).reshape(STEPS, rows_dev, width)
+
+
+def attend_steps(inputs, queries, new_keys, new_values, key_cache, value_cache, cache_lengths):
+    rows_dev = inputs.shape[1]
+    per_group = HEADS // KV_HEADS
+    key_rows = jnp.concatenate([key_cache, jnp.swapaxes(new_keys, 0, 1)], axis=1).reshape(
+        rows_dev, CACHE + STEPS, KV_HEADS, HEAD_DIM
+    )
+    value_rows = jnp.concatenate([value_cache, jnp.swapaxes(new_values, 0, 1)], axis=1).reshape(
+        rows_dev, CACHE + STEPS, KV_HEADS, HEAD_DIM
+    )
+    query_vals = queries.reshape(STEPS, rows_dev, KV_HEADS, per_group, HEAD_DIM)
+    scores = jnp.einsum(
+        "tbkgd,bjkd->bktgj", query_vals, key_rows, preferred_element_type=jnp.float32
+    ) * (HEAD_DIM ** (-0.5))
+    place = jnp.arange(CACHE + STEPS, dtype=jnp.int32)
+    step = jnp.arange(STEPS, dtype=jnp.int32)
+    ok_old = place[None, None, :] < cache_lengths[:, None, None]
+    ok_new = (place[None, :] >= CACHE) & (place[None, :] - CACHE <= step[:, None])
+    ok = ok_old & (place < CACHE) | ok_new[None]
+    scores = jnp.where(ok[:, None, :, None, :], scores, -1e30)
+    highest = jnp.max(scores, axis=-1, keepdims=True)
+    weights = jnp.exp(scores - highest)
+    probs = (weights / jnp.sum(weights, axis=-1, keepdims=True)).astype(jnp.bfloat16)
+    attended = jnp.einsum(
+        "bktgj,bjkd->tbkgd", probs, value_rows, preferred_element_type=jnp.float32
+    )
+    return (inputs.astype(jnp.float32) + attended.reshape(inputs.shape)).astype(jnp.bfloat16)
+
+
+def pick_plan(*args):
+    rows_dev = args[0].shape[1]
+    capacity = max(2, 2 * rows_dev * TOPK // lax.axis_size("expert"))
+    if capacity >= rows_dev:
+        return dense_shards(*args)
+    return shards(*args)
+
+
 def solution(mesh):
     in_specs = (
         P(None, ("group", "expert"), None),
@@ -138,4 +240,4 @@
         P("expert", None, "group"),
     )
     out_specs = P(None, ("group", "expert"), None)
-    return jax.shard_map(shards, mesh=mesh, in_specs=in_specs, out_specs=out_specs, check_vma=False)
+    return jax.shard_map(pick_plan, mesh=mesh, in_specs=in_specs, out_specs=out_specs, check_vma=False)

time: 221 us -> 209 us (0.946)
  blocking collectives: 0 us -> 42.3 us
  waiting for transfers between devices: 136 us -> 110 us
  starting transfers between devices: 29.8 us -> 5.04 us
  matrix products: 33.3 us -> 16.2 us
  local copies, waits for them, and re-layouts: 3.68 us -> 15.8 us
    reduce_scatter x0 -> x1, waiting for transfers between devices: none -> 102 us  [dense_shards(): lax.psum_scatter(weighted, ('group', 'expert'), scatter_dimension=0, tile...]
    all_gather x3 -> x1, waiting for transfers between devices: 86.2 us -> 1.1 us  [dense_shards(): tokens = lax.all_gather(flat, ('group', 'expert'), axis=0, tiled=True)]
    all_to_all x6 -> x0, waiting for transfers between devices: 47.5 us -> none  [the longest x3 25.4 us: shards(): lax.all_to_all(expert_out.reshape(num_slots, item_count, feature_dim), 'e...]
    all_gather x0 -> x1, blocking collectives: none -> 42.3 us  [dense_shards(): factors = lax.all_gather(mixing, ('group', 'expert'), axis=0, tiled=True)]
    all_to_all x6 -> x0, starting transfers between devices: 29.7 us -> none  [the longest x3 15.7 us: shards(): lax.all_to_all(outgoing, 'expert', split_axis=0, concat_axis=0, tiled=True)]
    dot_general x23 -> x3, matrix products: 33.3 us -> 14.5 us  [the longest x1 7.83 us: dense_shards(): jnp.dot(activated, down_full, preferred_element_type=jnp.float32)]
    ppermute x0 -> x3, waiting for transfers between devices: none -> 7.04 us  [dense_shards(): pieces = tuple((lax.ppermute(piece, 'group', perm) for piece in pieces))]
    ppermute x0 -> x3, starting transfers between devices: none -> 4.99 us  [dense_shards(): pieces = tuple((lax.ppermute(piece, 'group', perm) for piece in pieces))]
  transfers between devices with their start and end apart: 9 -> 5, of which waited for: 7 -> 3; matrix products, arithmetic and copies ran while one was open for 18% -> 4% of each run, Pallas kernels for 0% -> 0%
where the time goes in v1:
time: 209 us; the launch traced here: 208 us
  waiting for transfers between devices  110 us (53%)
  blocking collectives  42.3 us (20%)
  matrix products  16.2 us (8%)
  local copies, waits for them, and re-layouts  15.8 us (8%)
  between operations  13.7 us (7%)
  starting transfers between devices  5.04 us (2%)
  other arithmetic  4.92 us (2%)
    reduce_scatter x1, waiting for transfers between devices, dense_shards(): lax.psum_scatter(weighted, ('group', 'expert'), scatter_dimension=0, tile...  102 us
    all_gather x1, blocking collectives, dense_shards(): factors = lax.all_gather(mixing, ('group', 'expert'), axis=0, tiled=True)  42.3 us
    dot_general x1, matrix products, dense_shards(): jnp.dot(activated, down_full, preferred_element_type=jnp.float32)  7.83 us
    ppermute x3, waiting for transfers between devices, dense_shards(): pieces = tuple((lax.ppermute(piece, 'group', perm) for piece in pieces))  7.04 us
    unnamed x26, local copies, waits for them, and re-layouts  5.1 us
    ppermute x3, starting transfers between devices, dense_shards(): pieces = tuple((lax.ppermute(piece, 'group', perm) for piece in pieces))  4.99 us
    dot_general x1, matrix products, dense_shards(): gate_val = jnp.dot(tokens, gate_full, preferred_element_type=jnp.float32)  4.78 us
  transfers between devices with their start and end apart: 5, of which 3 were waited for; matrix products, arithmetic and copies ran while one was open for 4% of the time, Pallas kernels for 0%

profile of v1, /device:TPU:0, one launch (start us, length us, event | category | flops | bytes accessed | tf_op | source)
XLA Modules:
  0.0 208.0 jit_solution(6469075589126624056)
XLA Ops:
  6.6 0.7 copy.59
  7.3 0.7 copy.60
  8.0 1.1 reshape.120
  9.1 0.0 copy-start.7
  9.1 1.3 pad_maximum_fusion
  10.4 0.5 copy.40
  10.9 0.1 pad_maximum_fusion.1
  11.0 0.5 copy.42
  11.5 0.0 copy-done.10
  11.5 0.1 fusion.9
  11.7 1.7 fusion.18
  13.4 1.9 convolution_bitcast_fusion
  15.3 0.0 copy-start.1
  15.3 0.0 copy-start.2
  15.3 0.8 reshape.121
  16.2 1.8 fusion.5
  18.0 0.0 all-gather.3.cloned.1.call-update
  18.0 0.0 reduce-scatter.2.cloned.1.call-start
  18.1 1.0 dynamic-slice_bitcast_fusion.2
  19.0 3.0 %collective-permute-start = (bf16[1024,384]{1,0:T(8,128)(2,1)}, bf16[1024,384]{1,0:T(8,128)(2,1)}, u32[]{:S(2)}, u32[]{:S(2)}) collective-permute-start(bf16[1024,384]{1,0:T(8,128)(2,1)} %dynamic-slice_bitcast_fusion.2), channel_id=1, source_target_pairs={{0,16},{16,0},{1,17},{17,1},{2,18},{18,2},{3,19},{19,3},{4,20},{20... | collective-permute-start | bytes 2359304 | tf_op jit(solution)/shard_map/ppermute | solution.py:160
  22.0 1.0 dynamic-slice_bitcast_fusion
  23.0 0.0 collective-permute-start.2
  23.0 1.0 dynamic-slice_bitcast_fusion.1
  24.0 2.0 collective-permute-start.1
  26.0 0.1 select_reduce_fusion
  26.1 0.1 copy.45
  26.2 42.3 %all-gather = f32[32,24,16]{1,2,0:T(8,128)S(1)} all-gather(f32[1,24,16]{1,2,0:T(8,128)S(1)} %copy.45), channel_id=1, replica_groups=mesh['group'=2,'expert'=16] {'group','expert'}, dimensions={0}, use_global_device_ids=true | all-gather | bytes 50688 | tf_op jit(solution)/shard_map/all_gather | solution.py:179
  68.5 0.1 copy.46
  68.6 0.2 reshape.126
  68.8 0.1 broadcast.88.clone
  69.0 0.2 bitcast_dynamic-update-slice_fusion.2
  69.1 0.2 broadcast_in_dim.44
  69.3 1.1 copy-done.3
  70.4 0.1 bitcast_dynamic-update-slice_fusion
  70.5 0.1 broadcast.88.clone.1
  70.6 1.2 copy-done.5
  71.8 0.2 bitcast_dynamic-update-slice_fusion.1
  72.0 1.3 constant_dynamic-update-slice_fusion.2
  73.3 1.2 constant_dynamic-update-slice_fusion
  74.5 1.1 copy-done
  75.7 7.0 %collective-permute-done.1 = bf16[1024,384]{1,0:T(8,128)(2,1)} collective-permute-done((bf16[1024,384]{1,0:T(8,128)(2,1)}, bf16[1024,384]{1,0:T(8,128)(2,1)}, u32[]{:S(2)}, u32[]{:S(2)}) %collective-permute-start.1) | collective-permute-done | bytes 786464 | tf_op jit(solution)/shard_map/ppermute | solution.py:160
  82.7 1.3 constant_dynamic-update-slice_fusion.1
  84.0 1.1 all-gather.3.cloned.1.call-done
  85.1 4.8 %fusion.23 = f32[768,384]{1,0:T(8,128)} fusion(bf16[768,2048]{1,0:T(8,128)(2,1)} %all-gather.3.cloned.1.call-done, bf16[2048,384]{1,0:T(8,128)(2,1)S(1)} %constant_dynamic-update-slice_fusion.2), kind=kOutput, calls=%fused_computation.45 | convolution fusion | flops 1207959552 | bytes 5898240 | tf_op jit(solution)/shard_map/dot_general | solution.py:181
  89.9 7.8 %multiply_convert_fusion = bf16[768,2048]{1,0:T(8,128)(2,1)} fusion(bf16[384,2048]{1,0:T(8,128)(2,1)} %copy-done, f32[768]{0:T(1024)S(1)} %fusion.11, f32[768,384]{1,0:T(8,128)} %fusion.23, bf16[768,2048]{1,0:T(8,128)(2,1)} %all-gather.3.cloned.1.call-done, bf16[2048,384]{1,0:T(8,128)(2,1)S(1)} %constant_dynamic-update-slice_fusion.1), kind=kOutput, calls=%fused_computation.1 | convolution fusion | flops 2420834304 | bytes 10619904 | tf_op jit(solution)/shard_map/dot_general | solution.py:184
  97.7 0.0 reduce-scatter.2.cloned.1.call-update
  97.7 101.9 %reduce-scatter.2.cloned.1.call-done = bf16[24,2048]{1,0:T(8,128)(2,1)} async-done(((bf16[768,2048]{1,0:T(8,128)(2,1)}), bf16[24,2048]{1,0:T(8,128)(2,1)}) %reduce-scatter.2.cloned.1.call-update) | async-done | bytes 98320 | tf_op jit(solution)/shard_map/reduce_scatter | solution.py:186
  199.6 1.6 fusion.6
  (25 shorter events, 0.1 us)
Async XLA Ops:
  6.5 78.6 %all-gather.3.cloned.1.call-start = ((), (), s32[]{:S(2)}) async-start(), calls=%async_computation.1 | async-start | bytes 3244032 | tf_op jit(solution)/shard_map/all_gather | solution.py:178
  9.1 1.8 copy-start.7
  10.9 0.7 copy-start.10
  15.3 2.8 %copy-start.1 = (bf16[1,1024,768]{2,1,0:T(8,128)(2,1)S(1)}, bf16[1,1024,768]{2,1,0:T(8,128)(2,1)}, u32[]{:S(2)}) copy-start(bf16[1,1024,768]{2,1,0:T(8,128)(2,1)} %param.21) | copy-start | bytes 4718596
  15.3 6.7 %copy-start.2 = (bf16[1,768,1024]{2,1,0:T(8,128)(2,1)S(1)}, bf16[1,768,1024]{2,1,0:T(8,128)(2,1)}, u32[]{:S(2)}) copy-start(bf16[1,768,1024]{2,1,0:T(8,128)(2,1)} %param.23) | copy-start | bytes 4718596
  18.0 181.6 %reduce-scatter.2.cloned.1.call-start = ((), (), s32[]{:S(2)}) async-start(), calls=%async_computation.2 | async-start | bytes 3244032 | tf_op jit(solution)/shard_map/reduce_scatter | solution.py:186
  18.1 4.9 %copy-start.4 = (bf16[1,1024,768]{2,1,0:T(8,128)(2,1)S(1)}, bf16[1,1024,768]{2,1,0:T(8,128)(2,1)}, u32[]{:S(2)}) copy-start(bf16[1,1024,768]{2,1,0:T(8,128)(2,1)} %param.22) | copy-start | bytes 4718596
  19.0 6.9 %copy-start.8 = (f32[3,8,8]{2,1,0:T(8,128)S(1)}, f32[3,8,8]{2,1,0:T(8,128)}, u32[]{:S(2)}) copy-start(f32[3,8,8]{2,1,0:T(8,128)} %param.20) | copy-start | bytes 2308
  19.0 6.9 %copy-start.9 = (s32[3,8,8]{2,1,0:T(8,128)S(1)}, s32[3,8,8]{2,1,0:T(8,128)}, u32[]{:S(2)}) copy-start(s32[3,8,8]{2,1,0:T(8,128)} %param.19) | copy-start | bytes 2308
  19.0 52.9 %collective-permute-start = (bf16[1024,384]{1,0:T(8,128)(2,1)}, bf16[1024,384]{1,0:T(8,128)(2,1)}, u32[]{:S(2)}, u32[]{:S(2)}) collective-permute-start(bf16[1024,384]{1,0:T(8,128)(2,1)} %dynamic-slice_bitcast_fusion.2), channel_id=1, source_target_pairs={{0,16},{16,0},{1,17},{17,1},{2,18},{18,2},{3,19},{19,3},{4,20},{20... | collective-permute-start | bytes 2359304 | tf_op jit(solution)/shard_map/ppermute | solution.py:160
  23.0 50.3 %collective-permute-start.2 = (bf16[384,1024]{1,0:T(8,128)(2,1)}, bf16[384,1024]{1,0:T(8,128)(2,1)}, u32[]{:S(2)}, u32[]{:S(2)}) collective-permute-start(bf16[384,1024]{1,0:T(8,128)(2,1)} %dynamic-slice_bitcast_fusion), channel_id=1, source_target_pairs={{0,16},{16,0},{1,17},{17,1},{2,18},{18,2},{3,19},{19,3},{4,20},{20... | collective-permute-start | bytes 2359304 | tf_op jit(solution)/shard_map/ppermute | solution.py:160
  24.0 58.7 %collective-permute-start.1 = (bf16[1024,384]{1,0:T(8,128)(2,1)}, bf16[1024,384]{1,0:T(8,128)(2,1)}, u32[]{:S(2)}, u32[]{:S(2)}) collective-permute-start(bf16[1024,384]{1,0:T(8,128)(2,1)} %dynamic-slice_bitcast_fusion.1), channel_id=1, source_target_pairs={{0,16},{16,0},{1,17},{17,1},{2,18},{18,2},{3,19},{19,3},{4,20},{20... | collective-permute-start | bytes 2359304 | tf_op jit(solution)/shard_map/ppermute | solution.py:160
  69.0 1.4 copy-start.3
  70.4 1.4 copy-start.5
  74.5 1.1 copy-start
  97.7 101.9 %copy-start.6 = (bf16[24,2048]{1,0:T(8,128)(2,1)S(1)}, bf16[24,2048]{1,0:T(8,128)(2,1)}, u32[]{:S(2)}) copy-start(bf16[24,2048]{1,0:T(8,128)(2,1)} %fusion.5) | copy-start | bytes 294916
Sparse Core Ops, SparseCore 0:
  18.1 66.9 all-gather.2
  97.9 101.7 reduce-scatter.1

commit v2 on v1

--- a/solution.py
+++ b/solution.py
@@ -175,17 +175,55 @@
     )
     mixing = mixing.reshape(STEPS * rows_dev, experts_all)
     flat = hidden.reshape(STEPS * rows_dev, width)
-    tokens = lax.all_gather(flat, ("group", "expert"), axis=0, tiled=True)
-    factors = lax.all_gather(mixing, ("group", "expert"), axis=0, tiled=True)
+    tokens = gather_tree(flat).reshape(-1, width)
+    factors = gather_tree(mixing).reshape(-1, experts_all)
     factor = lax.dynamic_slice_in_dim(factors, lax.axis_index("expert"), 1, 1)
     gate_val = jnp.dot(tokens, gate_full, preferred_element_type=jnp.float32)
     up_val = jnp.dot(tokens, up_full, preferred_element_type=jnp.float32)
     activated = (jax.nn.silu(gate_val) * up_val).astype(jnp.bfloat16)
     expert_out = jnp.dot(activated, down_full, preferred_element_type=jnp.float32)
-    weighted = (factor * expert_out).astype(jnp.bfloat16)
-    combined = lax.psum_scatter(weighted, ("group", "expert"), scatter_dimension=0, tiled=True)
-    out = flat.astype(jnp.float32) + combined.astype(jnp.float32)
+    combined = scatter_tree(factor * expert_out, STEPS * rows_dev)
+    out = flat.astype(jnp.float32) + combined
     return out.astype(jnp.bfloat16).reshape(STEPS, rows_dev, width)
+
+
+def tree_stages():
+    stages = [("group", lax.axis_size("group"), 1)]
+    left = lax.axis_size("expert")
+    inner = []
+    stride = 1
+    while left % 2 == 0 and len(inner) < 2:
+        inner.append(("expert", 2, stride))
+        stride, left = 2 * stride, left // 2
+    if left > 1:
+        inner.append(("expert", left, stride))
+    return stages + inner[::-1]
+
+
+def shift_stage(value, stage, shift):
+    axis, size, stride = stage
+    perm = []
+    for i in range(lax.axis_size(axis)):
+        digit = i // stride % size
+        perm.append((i, i + ((digit + shift) % size - digit) * stride))
+    return lax.ppermute(value, axis, perm)
+
+
+def gather_tree(value):
+    for stage in tree_stages():
+        value = jnp.stack([value] + [shift_stage(value, stage, k) for k in range(1, stage[1])])
+    return value
+
+
+def scatter_tree(value, rows):
+    for stage in tree_stages()[::-1]:
+        value = value.reshape(stage[1], -1, value.shape[-1])
+        total = value[0]
+        for k in range(1, stage[1]):
+            arrived = shift_stage(value[k].astype(jnp.bfloat16), stage, -k)
+            total = total + arrived.astype(jnp.float32)
+        value = total
+    return value.reshape(rows, -1)
 
 
 def attend_steps(inputs, queries, new_keys, new_values, key_cache, value_cache, cache_lengths):

time: 209 us -> 180 us (0.86)
  blocking collectives: 42.3 us -> 0 us
  starting transfers between devices: 5.04 us -> 39.6 us
  between operations: 13.7 us -> 0.39 us
  waiting for transfers between devices: 110 us -> 97.5 us
  other arithmetic: 4.92 us -> 10.1 us
    reduce_scatter x1 -> x0, waiting for transfers between devices: 102 us -> none  [dense_shards(): lax.psum_scatter(weighted, ('group', 'expert'), scatter_dimension=0, tile...]
    ppermute x0 -> x18, waiting for transfers between devices: none -> 74.3 us  [shift_stage(): return lax.ppermute(value, axis, perm)]
    all_gather x1 -> x0, blocking collectives: 42.3 us -> none  [dense_shards(): factors = lax.all_gather(mixing, ('group', 'expert'), axis=0, tiled=True)]
    ppermute x0 -> x18, starting transfers between devices: none -> 36 us  [shift_stage(): return lax.ppermute(value, axis, perm)]
    ppermute x3, waiting for transfers between devices: 7.04 us -> 23.1 us  [dense_shards(): pieces = tuple((lax.ppermute(piece, 'group', perm) for piece in pieces))]
    another operation x0 -> x9, other arithmetic: none -> 5.29 us  [the longest x8 5.03 us: gather_tree(): jnp.stack([value] + [shift_stage(value, stage, k) for k in range(1, stage...]
    add x0 -> x2, other arithmetic: none -> 2.5 us  [scatter_tree(): total = total + arrived.astype(jnp.float32)]
    slice x0 -> x4, local copies, waits for them, and re-layouts: none -> 2.26 us  [scatter_tree(): arrived = shift_stage(value[k].astype(jnp.bfloat16), stage, -k)]
  transfers between devices with their start and end apart: 5 -> 21, of which waited for: 3 -> 16; matrix products, arithmetic and copies ran while one was open for 4% -> 7% of each run, Pallas kernels for 0% -> 0%
where the time goes in v2:
time: 180 us; the launch traced here: 179 us
  waiting for transfers between devices  97.5 us (54%)
  starting transfers between devices  39.6 us (22%)
  local copies, waits for them, and re-layouts  17.1 us (10%)
  matrix products  14.8 us (8%)
  other arithmetic  10.1 us (6%)
    ppermute x18, waiting for transfers between devices, shift_stage(): return lax.ppermute(value, axis, perm)  74.3 us
    ppermute x18, starting transfers between devices, shift_stage(): return lax.ppermute(value, axis, perm)  36 us
    ppermute x3, waiting for transfers between devices, dense_shards(): pieces = tuple((lax.ppermute(piece, 'group', perm) for piece in pieces))  23.1 us
    dot_general x1, matrix products, dense_shards(): jnp.dot(activated, down_full, preferred_element_type=jnp.float32)  8.28 us
    another operation x8, other arithmetic, gather_tree(): jnp.stack([value] + [shift_stage(value, stage, k) for k in range(1, stage...  5.03 us
    unnamed x36, local copies, waits for them, and re-layouts  3.8 us
  transfers between devices with their start and end apart: 21, of which 16 were waited for; matrix products, arithmetic and copies ran while one was open for 7% of the time, Pallas kernels for 0%

profile of v2, /device:TPU:0, one launch (start us, length us, event | category | flops | bytes accessed | tf_op | source)
XLA Modules:
  0.0 179.3 jit_solution(7954522877150745707)
XLA Ops:
  1.4 1.1 reshape.150
  2.5 1.3 pad_maximum_fusion.2
  5.1 1.8 fusion.28
  6.9 1.9 %convolution_bitcast_fusion = f32[3,8,2,16,64]{4,3,0,2,1:T(8,128)S(1)} fusion(bf16[8,387,2,64,1]{1,3,4,2,0:T(8,128)(2,1)S(1)} %bitcast.83, f32[8,2,3,16,387]{4,3,2,1,0:T(8,128)} %get-tuple-element.23, f32[8,2,3,16]{3,2,1,0:T(4,128)S(1)} %get-tuple-element.22), kind=kOutput, calls=%fused_computation.12 | convolution fusion | flops 38638080 | bytes 2181120 | tf_op jit(solution)/shard_map/bktgj,bjkd->tbkgd/dot_general | solution.py:251
  9.0 3.0 %collective-permute-start.6 = (bf16[24,2048]{1,0:T(8,128)(2,1)S(1)}, bf16[24,2048]{1,0:T(8,128)(2,1)S(1)}, u32[]{:S(2)}, u32[]{:S(2)}) collective-permute-start(bf16[24,2048]{1,0:T(8,128)(2,1)S(1)} %bitcast.85), channel_id=1, source_target_pairs={{0,16},{16,0},{1,17},{17,1},{2,18},{18,2},{3,19},{19,3},{4,20},{20... | collective-permute-start | bytes 294920 | tf_op jit(solution)/shard_map/ppermute | solution.py:209
  12.1 2.8 %collective-permute-done.6 = bf16[24,2048]{1,0:T(8,128)(2,1)S(1)} collective-permute-done((bf16[24,2048]{1,0:T(8,128)(2,1)S(1)}, bf16[24,2048]{1,0:T(8,128)(2,1)S(1)}, u32[]{:S(2)}, u32[]{:S(2)}) %collective-permute-start.6) | collective-permute-done | bytes 98336 | tf_op jit(solution)/shard_map/ppermute | solution.py:209
  14.9 3.0 %collective-permute-start.8 = (bf16[2,24,2048]{2,1,0:T(8,128)(2,1)S(1)}, bf16[2,24,2048]{2,1,0:T(8,128)(2,1)S(1)}, u32[]{:S(2)}, u32[]{:S(2)}) collective-permute-start(bf16[2,24,2048]{2,1,0:T(8,128)(2,1)S(1)} %get-tuple-element.15), channel_id=1, source_target_pairs={{0,8},{1,9},{2,10},{3,11},{4,12},{5,13},{6,14},{7,15},{8,0},{9,1},... | collective-permute-start | bytes 589832 | tf_op jit(solution)/shard_map/ppermute | solution.py:209
  17.9 1.6 collective-permute-start.7
  19.5 2.2 %collective-permute-start.9 = (bf16[2,24,2048]{2,1,0:T(8,128)(2,1)S(1)}, bf16[2,24,2048]{2,1,0:T(8,128)(2,1)S(1)}, u32[]{:S(2)}, u32[]{:S(2)}) collective-permute-start(bf16[2,24,2048]{2,1,0:T(8,128)(2,1)S(1)} %get-tuple-element.15), channel_id=1, source_target_pairs={{0,12},{1,13},{2,14},{3,15},{4,0},{5,1},{6,2},{7,3},{8,4},{9,5},{1... | collective-permute-start | bytes 589832 | tf_op jit(solution)/shard_map/ppermute | solution.py:209
  21.7 9.6 %collective-permute-done.8 = bf16[2,24,2048]{2,1,0:T(8,128)(2,1)S(1)} collective-permute-done((bf16[2,24,2048]{2,1,0:T(8,128)(2,1)S(1)}, bf16[2,24,2048]{2,1,0:T(8,128)(2,1)S(1)}, u32[]{:S(2)}, u32[]{:S(2)}) %collective-permute-start.8) | collective-permute-done | bytes 196640 | tf_op jit(solution)/shard_map/ppermute | solution.py:209
  31.3 0.7 collective-permute-done.9
  32.1 1.3 collective-permute-start.10
  33.5 1.6 collective-permute-start
  35.1 14.2 %collective-permute-done.10 = bf16[4,2,24,2048]{3,2,1,0:T(8,128)(2,1)S(1)} collective-permute-done((bf16[4,2,24,2048]{3,2,1,0:T(8,128)(2,1)S(1)}, bf16[4,2,24,2048]{3,2,1,0:T(8,128)(2,1)S(1)}, u32[]{:S(2)}, u32[]{:S(2)}) %collective-permute-start.10) | collective-permute-done | bytes 786464 | tf_op jit(solution)/shard_map/ppermute | solution.py:209
  49.3 1.4 fusion.24
  51.3 1.0 dynamic-slice_bitcast_fusion
  52.9 1.0 dynamic-slice_bitcast_fusion.2
  53.9 1.4 collective-permute-start.12
  55.2 7.2 %collective-permute-start.2 = (f32[2,24,16]{2,1,0:T(8,128)S(1)}, f32[2,24,16]{2,1,0:T(8,128)S(1)}, u32[]{:S(2)}, u32[]{:S(2)}) collective-permute-start(f32[2,24,16]{2,1,0:T(8,128)S(1)} %get-tuple-element.21), channel_id=1, source_target_pairs={{0,8},{1,9},{2,10},{3,11},{4,12},{5,13},{6,14},{7,15},{8,0},{9,1},... | collective-permute-start | bytes 9224 | tf_op jit(solution)/shard_map/ppermute | solution.py:209
  62.4 1.0 dynamic-slice_bitcast_fusion.1
  63.4 0.8 collective-permute-done.2
  64.2 3.0 %collective-permute-start.3 = (f32[2,24,16]{2,1,0:T(8,128)S(1)}, f32[2,24,16]{2,1,0:T(8,128)S(1)}, u32[]{:S(2)}, u32[]{:S(2)}) collective-permute-start(f32[2,24,16]{2,1,0:T(8,128)S(1)} %get-tuple-element.21), channel_id=1, source_target_pairs={{0,12},{1,13},{2,14},{3,15},{4,0},{5,1},{6,2},{7,3},{8,4},{9,5},{1... | collective-permute-start | bytes 9224 | tf_op jit(solution)/shard_map/ppermute | solution.py:209
  67.6 1.6 collective-permute-done.1
  69.2 1.5 collective-permute-start.13
  70.7 1.6 collective-permute-start.4
  72.6 2.8 %collective-permute-done.4 = f32[4,2,24,16]{3,2,1,0:T(8,128)S(1)} collective-permute-done((f32[4,2,24,16]{3,2,1,0:T(8,128)S(1)}, f32[4,2,24,16]{3,2,1,0:T(8,128)S(1)}, u32[]{:S(2)}, u32[]{:S(2)}) %collective-permute-start.4) | collective-permute-done | bytes 12320 | tf_op jit(solution)/shard_map/ppermute | solution.py:209
  76.4 1.4 collective-permute-done.5
  77.9 1.0 pad_maximum_fusion.5
  79.1 10.7 %collective-permute-done.12 = bf16[1024,384]{1,0:T(8,128)(2,1)} collective-permute-done((bf16[1024,384]{1,0:T(8,128)(2,1)}, bf16[1024,384]{1,0:T(8,128)(2,1)}, u32[]{:S(2)}, u32[]{:S(2)}) %collective-permute-start.12) | collective-permute-done | bytes 786464 | tf_op jit(solution)/shard_map/ppermute | solution.py:160
  89.8 2.1 %constant_dynamic-update-slice_fusion.2 = bf16[2048,384]{1,0:T(8,128)(2,1)} fusion(bf16[2048,384]{1,0:T(8,128)(2,1)} %copy-done.1, bf16[1024,384]{1,0:T(8,128)(2,1)} %collective-permute-done.12, s32[]{:T(128)S(6)} %select_n.37), kind=kLoop, calls=%fused_computation.51 | loop fusion | bytes 1572868 | tf_op jit(solution)/shard_map/dynamic_update_slice | solution.py:163
  91.9 1.2 constant_dynamic-update-slice_fusion
  93.1 12.5 %collective-permute-done.13 = bf16[1024,384]{1,0:T(8,128)(2,1)} collective-permute-done((bf16[1024,384]{1,0:T(8,128)(2,1)}, bf16[1024,384]{1,0:T(8,128)(2,1)}, u32[]{:S(2)}, u32[]{:S(2)}) %collective-permute-start.13) | collective-permute-done | bytes 786464 | tf_op jit(solution)/shard_map/ppermute | solution.py:160
  105.6 1.3 constant_dynamic-update-slice_fusion.1
  106.9 1.8 %pad_maximum_fusion = bf16[2,2,4,2,24,2048]{5,4,3,2,1,0:T(8,128)(2,1)S(1)} fusion(bf16[1,2,4,2,24,2048]{5,4,3,2,1,0:T(8,128)(2,1)} %bitcast.32, bf16[1,2,4,2,24,2048]{5,4,3,2,1,0:T(8,128)(2,1)S(1)} %get-tuple-element.7), kind=kLoop, calls=%fused_computation.4 | loop fusion | flops 1572864 | bytes 6291456 | tf_op jit(solution)/shard_map/stack | solution.py:214
  108.8 1.7 copy-done
  110.5 2.8 %fusion.33 = f32[768,384]{1,0:T(8,128)} fusion(bf16[768,2048]{1,0:T(8,128)(2,1)S(1)} %bitcast.80, bf16[2048,384]{1,0:T(8,128)(2,1)S(1)} %copy-done.2), kind=kOutput, calls=%fused_computation.69 | convolution fusion | flops 1207959552 | bytes 5898240 | tf_op jit(solution)/shard_map/dot_general | solution.py:181
  113.3 8.3 %convolution_multiply_fusion = f32[768,2048]{1,0:T(8,128)} fusion(bf16[384,2048]{1,0:T(8,128)(2,1)S(1)} %copy-done.6, f32[768]{0:T(1024)S(1)} %dynamic-slice_reduce_fusion, f32[768,384]{1,0:T(8,128)} %fusion.33, bf16[768,2048]{1,0:T(8,128)(2,1)} %bitcast.81, bf16[2048,384]{1,0:T(8,128)(2,1)S(1)} %constant_dynamic-update-slice_fusion.1), kind=kOutput, calls=%fused_computation.1 | convolution fusion | flops 2419261440 | bytes 13765632 | tf_op jit(solution)/shard_map/dot_general | solution.py:184
  121.6 2.1 %slice.83 = bf16[384,2048]{1,0:T(8,128)(2,1)S(1)} slice(f32[768,2048]{1,0:T(8,128)} %convolution_multiply_fusion), slice={[384:768], [0:2048]} | slice | bytes 3145728 | tf_op jit(solution)/shard_map/slice | solution.py:223
  123.8 3.4 %collective-permute-done.15 = bf16[384,2048]{1,0:T(8,128)(2,1)S(1)} collective-permute-done((bf16[384,2048]{1,0:T(8,128)(2,1)S(1)}, bf16[384,2048]{1,0:T(8,128)(2,1)S(1)}, u32[]{:S(2)}, u32[]{:S(2)}) %collective-permute-start.15) | collective-permute-done | bytes 1572896 | tf_op jit(solution)/shard_map/ppermute | solution.py:209
  127.2 2.4 %slice_add_fusion = f32[384,2048]{1,0:T(8,128)S(1)} fusion(f32[768,2048]{1,0:T(8,128)} %convolution_multiply_fusion, bf16[384,2048]{1,0:T(8,128)(2,1)S(1)} %collective-permute-done.15), kind=kLoop, calls=%fused_computation.3 | loop fusion | flops 1572864 | bytes 7864320 | tf_op jit(solution)/shard_map/add | solution.py:224
  130.4 18.9 %collective-permute-done.16 = bf16[192,2048]{1,0:T(8,128)(2,1)S(1)} collective-permute-done((bf16[192,2048]{1,0:T(8,128)(2,1)S(1)}, bf16[192,2048]{1,0:T(8,128)(2,1)S(1)}, u32[]{:S(2)}, u32[]{:S(2)}) %collective-permute-start.16) | collective-permute-done | bytes 786464 | tf_op jit(solution)/shard_map/ppermute | solution.py:209
  149.6 1.7 collective-permute-start.17
  151.3 3.7 %collective-permute-start.19 = (bf16[48,2048]{1,0:T(8,128)(2,1)S(1)}, bf16[48,2048]{1,0:T(8,128)(2,1)S(1)}, u32[]{:S(2)}, u32[]{:S(2)}) collective-permute-start(bf16[48,2048]{1,0:T(8,128)(2,1)S(1)} %get-tuple-element.10), channel_id=1, source_target_pairs={{0,4},{1,5},{2,6},{3,7},{4,8},{5,9},{6,10},{7,11},{8,12},{9,13},{1... | collective-permute-start | bytes 589832 | tf_op jit(solution)/shard_map/ppermute | solution.py:209
  155.0 3.9 %collective-permute-start.18 = (bf16[48,2048]{1,0:T(8,128)(2,1)S(1)}, bf16[48,2048]{1,0:T(8,128)(2,1)S(1)}, u32[]{:S(2)}, u32[]{:S(2)}) collective-permute-start(bf16[48,2048]{1,0:T(8,128)(2,1)S(1)} %get-tuple-element.11), channel_id=1, source_target_pairs={{0,8},{1,9},{2,10},{3,11},{4,12},{5,13},{6,14},{7,15},{8,0},{9,1},... | collective-permute-start | bytes 589832 | tf_op jit(solution)/shard_map/ppermute | solution.py:209
  159.3 9.1 %collective-permute-done.19 = bf16[48,2048]{1,0:T(8,128)(2,1)S(1)} collective-permute-done((bf16[48,2048]{1,0:T(8,128)(2,1)S(1)}, bf16[48,2048]{1,0:T(8,128)(2,1)S(1)}, u32[]{:S(2)}, u32[]{:S(2)}) %collective-permute-start.19) | collective-permute-done | bytes 196640 | tf_op jit(solution)/shard_map/ppermute | solution.py:209
  168.4 5.4 %collective-permute-done.18 = bf16[48,2048]{1,0:T(8,128)(2,1)S(1)} collective-permute-done((bf16[48,2048]{1,0:T(8,128)(2,1)S(1)}, bf16[48,2048]{1,0:T(8,128)(2,1)S(1)}, u32[]{:S(2)}, u32[]{:S(2)}) %collective-permute-start.18) | collective-permute-done | bytes 196640 | tf_op jit(solution)/shard_map/ppermute | solution.py:209
  174.0 1.6 collective-permute-start.20
  175.6 3.1 %collective-permute-done.20 = bf16[24,2048]{1,0:T(8,128)(2,1)S(1)} collective-permute-done((bf16[24,2048]{1,0:T(8,128)(2,1)S(1)}, bf16[24,2048]{1,0:T(8,128)(2,1)S(1)}, u32[]{:S(2)}, u32[]{:S(2)}) %collective-permute-start.20) | collective-permute-done | bytes 98336 | tf_op jit(solution)/shard_map/ppermute | solution.py:209
  (78 shorter events, 8.8 us)
Async XLA Ops:
  2.5 1.8 %copy-start.12 = (bf16[8,384,128]{2,1,0:T(8,128)(2,1)S(1)}, bf16[8,384,128]{2,1,0:T(8,128)(2,1)}, u32[]{:S(2)}) copy-start(bf16[8,384,128]{2,1,0:T(8,128)(2,1)} %param.16) | copy-start | bytes 2359300
  4.3 0.7 copy-start.16
  6.9 2.1 %copy-start.13 = (bf16[3,8,2048]{2,1,0:T(8,128)(2,1)S(1)}, bf16[3,8,2048]{2,1,0:T(8,128)(2,1)}, u32[]{:S(2)}) copy-start(bf16[3,8,2048]{2,1,0:T(8,128)(2,1)} %param.12) | copy-start | bytes 294916
  9.0 24.4 %copy-start.14 = (f32[3,8,8]{2,1,0:T(8,128)S(1)}, f32[3,8,8]{2,1,0:T(8,128)}, u32[]{:S(2)}) copy-start(f32[3,8,8]{2,1,0:T(8,128)} %param.20) | copy-start | bytes 2308
  9.0 24.4 %copy-start.15 = (s32[3,8,8]{2,1,0:T(8,128)S(1)}, s32[3,8,8]{2,1,0:T(8,128)}, u32[]{:S(2)}) copy-start(s32[3,8,8]{2,1,0:T(8,128)} %param.19) | copy-start | bytes 2308
  9.0 5.8 %collective-permute-start.6 = (bf16[24,2048]{1,0:T(8,128)(2,1)S(1)}, bf16[24,2048]{1,0:T(8,128)(2,1)S(1)}, u32[]{:S(2)}, u32[]{:S(2)}) collective-permute-start(bf16[24,2048]{1,0:T(8,128)(2,1)S(1)} %bitcast.85), channel_id=1, source_target_pairs={{0,16},{16,0},{1,17},{17,1},{2,18},{18,2},{3,19},{19,3},{4,20},{20... | collective-permute-start | bytes 294920 | tf_op jit(solution)/shard_map/ppermute | solution.py:209
  14.9 16.4 %collective-permute-start.8 = (bf16[2,24,2048]{2,1,0:T(8,128)(2,1)S(1)}, bf16[2,24,2048]{2,1,0:T(8,128)(2,1)S(1)}, u32[]{:S(2)}, u32[]{:S(2)}) collective-permute-start(bf16[2,24,2048]{2,1,0:T(8,128)(2,1)S(1)} %get-tuple-element.15), channel_id=1, source_target_pairs={{0,8},{1,9},{2,10},{3,11},{4,12},{5,13},{6,14},{7,15},{8,0},{9,1},... | collective-permute-start | bytes 589832 | tf_op jit(solution)/shard_map/ppermute | solution.py:209
  17.9 13.4 %collective-permute-start.7 = (bf16[2,24,2048]{2,1,0:T(8,128)(2,1)S(1)}, bf16[2,24,2048]{2,1,0:T(8,128)(2,1)S(1)}, u32[]{:S(2)}, u32[]{:S(2)}) collective-permute-start(bf16[2,24,2048]{2,1,0:T(8,128)(2,1)S(1)} %get-tuple-element.15), channel_id=1, source_target_pairs={{0,4},{1,5},{2,6},{3,7},{4,8},{5,9},{6,10},{7,11},{8,12},{9,13},{1... | collective-permute-start | bytes 589832 | tf_op jit(solution)/shard_map/ppermute | solution.py:209
  19.5 12.5 %collective-permute-start.9 = (bf16[2,24,2048]{2,1,0:T(8,128)(2,1)S(1)}, bf16[2,24,2048]{2,1,0:T(8,128)(2,1)S(1)}, u32[]{:S(2)}, u32[]{:S(2)}) collective-permute-start(bf16[2,24,2048]{2,1,0:T(8,128)(2,1)S(1)} %get-tuple-element.15), channel_id=1, source_target_pairs={{0,12},{1,13},{2,14},{3,15},{4,0},{5,1},{6,2},{7,3},{8,4},{9,5},{1... | collective-permute-start | bytes 589832 | tf_op jit(solution)/shard_map/ppermute | solution.py:209
  32.1 17.2 %collective-permute-start.10 = (bf16[4,2,24,2048]{3,2,1,0:T(8,128)(2,1)S(1)}, bf16[4,2,24,2048]{3,2,1,0:T(8,128)(2,1)S(1)}, u32[]{:S(2)}, u32[]{:S(2)}) collective-permute-start(bf16[4,2,24,2048]{3,2,1,0:T(8,128)(2,1)S(1)} %get-tuple-element.13), channel_id=1, source_target_pairs={{0,2},{1,3},{2,0},{3,1},{4,6},{5,7},{6,4},{7,5},{8,10},{9,11},{10,... | collective-permute-start | bytes 2359304 | tf_op jit(solution)/shard_map/ppermute | solution.py:209
  33.5 21.7 %collective-permute-start = (f32[24,16]{1,0:T(8,128)S(1)}, f32[24,16]{1,0:T(8,128)S(1)}, u32[]{:S(2)}, u32[]{:S(2)}) collective-permute-start(f32[24,16]{1,0:T(8,128)S(1)} %bitcast.93), channel_id=1, source_target_pairs={{0,16},{16,0},{1,17},{17,1},{2,18},{18,2},{3,19},{19,3},{4,20},{20... | collective-permute-start | bytes 4616 | tf_op jit(solution)/shard_map/ppermute | solution.py:209
  49.3 2.0 %copy-start.8 = (bf16[1,768,1024]{2,1,0:T(8,128)(2,1)S(1)}, bf16[1,768,1024]{2,1,0:T(8,128)(2,1)}, u32[]{:S(2)}) copy-start(bf16[1,768,1024]{2,1,0:T(8,128)(2,1)} %param.23) | copy-start | bytes 4718596
  50.7 2.2 %copy-start.7 = (bf16[1,1024,768]{2,1,0:T(8,128)(2,1)S(1)}, bf16[1,1024,768]{2,1,0:T(8,128)(2,1)}, u32[]{:S(2)}) copy-start(bf16[1,1024,768]{2,1,0:T(8,128)(2,1)} %param.21) | copy-start | bytes 4718596
  50.7 11.8 %copy-start.10 = (bf16[1,1024,768]{2,1,0:T(8,128)(2,1)S(1)}, bf16[1,1024,768]{2,1,0:T(8,128)(2,1)}, u32[]{:S(2)}) copy-start(bf16[1,1024,768]{2,1,0:T(8,128)(2,1)} %param.22) | copy-start | bytes 4718596
  50.7 56.3 %collective-permute-start.11 = (bf16[2,4,2,24,2048]{4,3,2,1,0:T(8,128)(2,1)}, bf16[2,4,2,24,2048]{4,3,2,1,0:T(8,128)(2,1)}, u32[]{:S(2)}, u32[]{:S(2)}) collective-permute-start(bf16[2,4,2,24,2048]{4,3,2,1,0:T(8,128)(2,1)} %get-tuple-element.8), channel_id=1, source_target_pairs={{0,1},{1,0},{2,3},{3,2},{4,5},{5,4},{6,7},{7,6},{8,9},{9,8},{10,11... | collective-permute-start | bytes 4718600 | tf_op jit(solution)/shard_map/ppermute | solution.py:209
  52.2 39.7 %collective-permute-start.14 = (bf16[384,1024]{1,0:T(8,128)(2,1)}, bf16[384,1024]{1,0:T(8,128)(2,1)}, u32[]{:S(2)}, u32[]{:S(2)}) collective-permute-start(bf16[384,1024]{1,0:T(8,128)(2,1)} %dynamic-slice_bitcast_fusion), channel_id=1, source_target_pairs={{0,16},{16,0},{1,17},{17,1},{2,18},{18,2},{3,19},{19,3},{4,20},{20... | collective-permute-start | bytes 2359304 | tf_op jit(solution)/shard_map/ppermute | solution.py:160
  53.9 35.9 %collective-permute-start.12 = (bf16[1024,384]{1,0:T(8,128)(2,1)}, bf16[1024,384]{1,0:T(8,128)(2,1)}, u32[]{:S(2)}, u32[]{:S(2)}) collective-permute-start(bf16[1024,384]{1,0:T(8,128)(2,1)} %dynamic-slice_bitcast_fusion.2), channel_id=1, source_target_pairs={{0,16},{16,0},{1,17},{17,1},{2,18},{18,2},{3,19},{19,3},{4,20},{20... | collective-permute-start | bytes 2359304 | tf_op jit(solution)/shard_map/ppermute | solution.py:160
  55.2 9.0 %collective-permute-start.2 = (f32[2,24,16]{2,1,0:T(8,128)S(1)}, f32[2,24,16]{2,1,0:T(8,128)S(1)}, u32[]{:S(2)}, u32[]{:S(2)}) collective-permute-start(f32[2,24,16]{2,1,0:T(8,128)S(1)} %get-tuple-element.21), channel_id=1, source_target_pairs={{0,8},{1,9},{2,10},{3,11},{4,12},{5,13},{6,14},{7,15},{8,0},{9,1},... | collective-permute-start | bytes 9224 | tf_op jit(solution)/shard_map/ppermute | solution.py:209
  63.4 5.7 %collective-permute-start.1 = (f32[2,24,16]{2,1,0:T(8,128)S(1)}, f32[2,24,16]{2,1,0:T(8,128)S(1)}, u32[]{:S(2)}, u32[]{:S(2)}) collective-permute-start(f32[2,24,16]{2,1,0:T(8,128)S(1)} %get-tuple-element.21), channel_id=1, source_target_pairs={{0,4},{1,5},{2,6},{3,7},{4,8},{5,9},{6,10},{7,11},{8,12},{9,13},{1... | collective-permute-start | bytes 9224 | tf_op jit(solution)/shard_map/ppermute | solution.py:209
  64.2 6.4 %collective-permute-start.3 = (f32[2,24,16]{2,1,0:T(8,128)S(1)}, f32[2,24,16]{2,1,0:T(8,128)S(1)}, u32[]{:S(2)}, u32[]{:S(2)}) collective-permute-start(f32[2,24,16]{2,1,0:T(8,128)S(1)} %get-tuple-element.21), channel_id=1, source_target_pairs={{0,12},{1,13},{2,14},{3,15},{4,0},{5,1},{6,2},{7,3},{8,4},{9,5},{1... | collective-permute-start | bytes 9224 | tf_op jit(solution)/shard_map/ppermute | solution.py:209
  67.4 5.0 %copy-start.9 = (bf16[1,768,1024]{2,1,0:T(8,128)(2,1)S(1)}, bf16[1,768,1024]{2,1,0:T(8,128)(2,1)}, u32[]{:S(2)}) copy-start(bf16[1,768,1024]{2,1,0:T(8,128)(2,1)} %param.23) | copy-start | bytes 4718596
  67.6 5.0 %copy-start.1 = (bf16[2048,384]{1,0:T(8,128)(2,1)}, bf16[2048,384]{1,0:T(8,128)(2,1)S(1)}, u32[]{:S(2)}) copy-start(bf16[2048,384]{1,0:T(8,128)(2,1)S(1)} %bitcast_dynamic-update-slice_fusion.2) | copy-start | bytes 4718596
  69.2 36.4 %collective-permute-start.13 = (bf16[1024,384]{1,0:T(8,128)(2,1)}, bf16[1024,384]{1,0:T(8,128)(2,1)}, u32[]{:S(2)}, u32[]{:S(2)}) collective-permute-start(bf16[1024,384]{1,0:T(8,128)(2,1)} %dynamic-slice_bitcast_fusion.1), channel_id=1, source_target_pairs={{0,16},{16,0},{1,17},{17,1},{2,18},{18,2},{3,19},{19,3},{4,20},{20... | collective-permute-start | bytes 2359304 | tf_op jit(solution)/shard_map/ppermute | solution.py:160
  70.7 4.7 %collective-permute-start.4 = (f32[4,2,24,16]{3,2,1,0:T(8,128)S(1)}, f32[4,2,24,16]{3,2,1,0:T(8,128)S(1)}, u32[]{:S(2)}, u32[]{:S(2)}) collective-permute-start(f32[4,2,24,16]{3,2,1,0:T(8,128)S(1)} %get-tuple-element.19), channel_id=1, source_target_pairs={{0,2},{1,3},{2,0},{3,1},{4,6},{5,7},{6,4},{7,5},{8,10},{9,11},{10,... | collective-permute-start | bytes 36872 | tf_op jit(solution)/shard_map/ppermute | solution.py:209
  72.5 3.8 %copy-start.11 = (bf16[1,1024,768]{2,1,0:T(8,128)(2,1)S(1)}, bf16[1,1024,768]{2,1,0:T(8,128)(2,1)}, u32[]{:S(2)}) copy-start(bf16[1,1024,768]{2,1,0:T(8,128)(2,1)} %param.22) | copy-start | bytes 4718596
  72.6 3.5 %copy-start.3 = (bf16[384,2048]{1,0:T(8,128)(2,1)}, bf16[384,2048]{1,0:T(8,128)(2,1)S(1)}, u32[]{:S(2)}) copy-start(bf16[384,2048]{1,0:T(8,128)(2,1)S(1)} %bitcast_dynamic-update-slice_fusion) | copy-start | bytes 4718596
  76.1 1.8 collective-permute-start.5
  76.4 15.5 %copy-start.4 = (bf16[384,2048]{1,0:T(8,128)(2,1)S(1)}, bf16[384,2048]{1,0:T(8,128)(2,1)}, u32[]{:S(2)}) copy-start(bf16[384,2048]{1,0:T(8,128)(2,1)} %copy-done.3) | copy-start | bytes 4718596
  93.1 13.8 %copy-start.5 = (bf16[384,2048]{1,0:T(8,128)(2,1)}, bf16[384,2048]{1,0:T(8,128)(2,1)S(1)}, u32[]{:S(2)}) copy-start(bf16[384,2048]{1,0:T(8,128)(2,1)S(1)} %constant_dynamic-update-slice_fusion) | copy-start | bytes 4718596
  106.9 3.6 %copy-start.2 = (bf16[2048,384]{1,0:T(8,128)(2,1)S(1)}, bf16[2048,384]{1,0:T(8,128)(2,1)}, u32[]{:S(2)}) copy-start(bf16[2048,384]{1,0:T(8,128)(2,1)} %constant_dynamic-update-slice_fusion.2) | copy-start | bytes 4718596
  108.8 1.7 copy-start
  110.5 2.8 %copy-start.6 = (bf16[384,2048]{1,0:T(8,128)(2,1)S(1)}, bf16[384,2048]{1,0:T(8,128)(2,1)}, u32[]{:S(2)}) copy-start(bf16[384,2048]{1,0:T(8,128)(2,1)} %copy-done.5) | copy-start | bytes 4718596
  123.7 3.5 %collective-permute-start.15 = (bf16[384,2048]{1,0:T(8,128)(2,1)S(1)}, bf16[384,2048]{1,0:T(8,128)(2,1)S(1)}, u32[]{:S(2)}, u32[]{:S(2)}) collective-permute-start(bf16[384,2048]{1,0:T(8,128)(2,1)S(1)} %slice.83), channel_id=1, source_target_pairs={{0,1},{1,0},{2,3},{3,2},{4,5},{5,4},{6,7},{7,6},{8,9},{9,8},{10,11... | collective-permute-start | bytes 4718600 | tf_op jit(solution)/shard_map/ppermute | solution.py:209
  129.7 19.6 %collective-permute-start.16 = (bf16[192,2048]{1,0:T(8,128)(2,1)S(1)}, bf16[192,2048]{1,0:T(8,128)(2,1)S(1)}, u32[]{:S(2)}, u32[]{:S(2)}) collective-permute-start(bf16[192,2048]{1,0:T(8,128)(2,1)S(1)} %slice.84), channel_id=1, source_target_pairs={{0,2},{1,3},{2,0},{3,1},{4,6},{5,7},{6,4},{7,5},{8,10},{9,11},{10,... | collective-permute-start | bytes 2359304 | tf_op jit(solution)/shard_map/ppermute | solution.py:209
  149.6 9.6 %collective-permute-start.17 = (bf16[48,2048]{1,0:T(8,128)(2,1)S(1)}, bf16[48,2048]{1,0:T(8,128)(2,1)S(1)}, u32[]{:S(2)}, u32[]{:S(2)}) collective-permute-start(bf16[48,2048]{1,0:T(8,128)(2,1)S(1)} %get-tuple-element.9), channel_id=1, source_target_pairs={{0,12},{1,13},{2,14},{3,15},{4,0},{5,1},{6,2},{7,3},{8,4},{9,5},{1... | collective-permute-start | bytes 589832 | tf_op jit(solution)/shard_map/ppermute | solution.py:209
  151.3 17.1 %collective-permute-start.19 = (bf16[48,2048]{1,0:T(8,128)(2,1)S(1)}, bf16[48,2048]{1,0:T(8,128)(2,1)S(1)}, u32[]{:S(2)}, u32[]{:S(2)}) collective-permute-start(bf16[48,2048]{1,0:T(8,128)(2,1)S(1)} %get-tuple-element.10), channel_id=1, source_target_pairs={{0,4},{1,5},{2,6},{3,7},{4,8},{5,9},{6,10},{7,11},{8,12},{9,13},{1... | collective-permute-start | bytes 589832 | tf_op jit(solution)/shard_map/ppermute | solution.py:209
  155.0 18.9 %collective-permute-start.18 = (bf16[48,2048]{1,0:T(8,128)(2,1)S(1)}, bf16[48,2048]{1,0:T(8,128)(2,1)S(1)}, u32[]{:S(2)}, u32[]{:S(2)}) collective-permute-start(bf16[48,2048]{1,0:T(8,128)(2,1)S(1)} %get-tuple-element.11), channel_id=1, source_target_pairs={{0,8},{1,9},{2,10},{3,11},{4,12},{5,13},{6,14},{7,15},{8,0},{9,1},... | collective-permute-start | bytes 589832 | tf_op jit(solution)/shard_map/ppermute | solution.py:209
  174.0 4.7 %collective-permute-start.20 = (bf16[24,2048]{1,0:T(8,128)(2,1)S(1)}, bf16[24,2048]{1,0:T(8,128)(2,1)S(1)}, u32[]{:S(2)}, u32[]{:S(2)}) collective-permute-start(bf16[24,2048]{1,0:T(8,128)(2,1)S(1)} %slice.85), channel_id=1, source_target_pairs={{0,16},{16,0},{1,17},{17,1},{2,18},{18,2},{3,19},{19,3},{4,20},{20... | collective-permute-start | bytes 294920 | tf_op jit(solution)/shard_map/ppermute | solution.py:209

commit v3 on v2

--- a/solution.py
+++ b/solution.py
@@ -144,9 +144,6 @@
     part = w_gate.shape[2] // groups
     depth = w_gate.shape[1]
     columns = w_down.shape[2]
-    gate_full = jnp.zeros((width, part), w_gate.dtype)
-    up_full = jnp.zeros((width, part), w_gate.dtype)
-    down_full = jnp.zeros((part, width), w_gate.dtype)
     pairs = []
     for shift in range(groups):
         target = lax.rem(me + shift, groups)
@@ -159,10 +156,6 @@
             perm = [(i, (i + shift) % groups) for i in range(groups)]
             pieces = tuple(lax.ppermute(piece, "group", perm) for piece in pieces)
         pairs.append((lax.rem(me - shift + groups, groups), pieces))
-    for source, (gate_piece, up_piece, down_piece) in pairs:
-        gate_full = lax.dynamic_update_slice_in_dim(gate_full, gate_piece, source * depth, 0)
-        up_full = lax.dynamic_update_slice_in_dim(up_full, up_piece, source * depth, 0)
-        down_full = lax.dynamic_update_slice_in_dim(down_full, down_piece, source * columns, 1)
     hidden = attend_steps(
         inputs, queries, new_keys, new_values, key_cache, value_cache, cache_lengths
     )
@@ -175,14 +168,39 @@
     )
     mixing = mixing.reshape(STEPS * rows_dev, experts_all)
     flat = hidden.reshape(STEPS * rows_dev, width)
-    tokens = gather_tree(flat).reshape(-1, width)
     factors = gather_tree(mixing).reshape(-1, experts_all)
     factor = lax.dynamic_slice_in_dim(factors, lax.axis_index("expert"), 1, 1)
-    gate_val = jnp.dot(tokens, gate_full, preferred_element_type=jnp.float32)
-    up_val = jnp.dot(tokens, up_full, preferred_element_type=jnp.float32)
+    stages = tree_stages()
+    arriving = [piece for k in range(1, groups) for piece in pairs[k][1]]
+    tokens = flat
+    for number, stage in enumerate(stages):
+        if number >= 2 and number - 2 < len(arriving):
+            tokens, arriving[number - 2] = lax.optimization_barrier((tokens, arriving[number - 2]))
+        tokens = gather_stage(tokens, stage)
+    tokens = tokens.reshape(-1, width)
+    gate_val, up_val, downs = 0.0, 0.0, []
+    for k in range(groups):
+        source, pieces = pairs[k]
+        if k:
+            pieces = arriving[3 * (k - 1) : 3 * k]
+        share = lax.dynamic_slice_in_dim(tokens, source * depth, depth, 1)
+        gate_val = gate_val + jnp.dot(share, pieces[0], preferred_element_type=jnp.float32)
+        up_val = up_val + jnp.dot(share, pieces[1], preferred_element_type=jnp.float32)
+        downs.append(pieces[2])
     activated = (jax.nn.silu(gate_val) * up_val).astype(jnp.bfloat16)
-    expert_out = jnp.dot(activated, down_full, preferred_element_type=jnp.float32)
-    combined = scatter_tree(factor * expert_out, STEPS * rows_dev)
+    expert_out = jnp.dot(
+        activated, jnp.concatenate(downs, axis=1), preferred_element_type=jnp.float32
+    )
+    combined = scatter_tree(factor * expert_out, stages[1:])
+    combined = combined.reshape(-1, groups, columns)
+    combined = jnp.concatenate(
+        [
+            lax.dynamic_index_in_dim(combined, lax.rem(me - at + groups, groups), 1, keepdims=False)
+            for at in range(groups)
+        ],
+        axis=1,
+    )
+    combined = scatter_tree(combined, stages[:1]).reshape(STEPS * rows_dev, width)
     out = flat.astype(jnp.float32) + combined
     return out.astype(jnp.bfloat16).reshape(STEPS, rows_dev, width)
 
@@ -209,21 +227,25 @@
     return lax.ppermute(value, axis, perm)
 
 
+def gather_stage(value, stage):
+    return jnp.stack([value] + [shift_stage(value, stage, k) for k in range(1, stage[1])])
+
+
 def gather_tree(value):
     for stage in tree_stages():
-        value = jnp.stack([value] + [shift_stage(value, stage, k) for k in range(1, stage[1])])
+        value = gather_stage(value, stage)
     return value
 
 
-def scatter_tree(value, rows):
-    for stage in tree_stages()[::-1]:
+def scatter_tree(value, stages):
+    for stage in stages[::-1]:
         value = value.reshape(stage[1], -1, value.shape[-1])
         total = value[0]
         for k in range(1, stage[1]):
             arrived = shift_stage(value[k].astype(jnp.bfloat16), stage, -k)
             total = total + arrived.astype(jnp.float32)
         value = total
-    return value.reshape(rows, -1)
+    return value
 
 
 def attend_steps(inputs, queries, new_keys, new_values, key_cache, value_cache, cache_lengths):

time: 180 us -> 169 us (0.939)
  local copies, waits for them, and re-layouts: 17.1 us -> 11.9 us
  starting transfers between devices: 39.6 us -> 35.5 us
  waiting for transfers between devices: 97.5 us -> 94.6 us
  matrix products: 14.8 us -> 17.5 us
    ppermute x3, waiting for transfers between devices: 23.1 us -> 12.5 us  [dense_shards(): pieces = tuple((lax.ppermute(piece, 'group', perm) for piece in pieces))]
    ppermute x18, waiting for transfers between devices: 74.3 us -> 82.2 us  [shift_stage(): return lax.ppermute(value, axis, perm)]
    ppermute x18, starting transfers between devices: 36 us -> 29.4 us  [shift_stage(): return lax.ppermute(value, axis, perm)]
    dynamic_update_slice x6 -> x0, local copies, waits for them, and re-layouts: 5 us -> none  [the longest x2 2.28 us: dense_shards(): lax.dynamic_update_slice_in_dim(gate_full, gate_piece, source * depth, 0)]
    unnamed x36 -> x35, local copies, waits for them, and re-layouts: 3.8 us -> 0.15 us
    ppermute x3, starting transfers between devices: 3.54 us -> 6.08 us  [dense_shards(): pieces = tuple((lax.ppermute(piece, 'group', perm) for piece in pieces))]
    another operation x9 -> x10, other arithmetic: 5.29 us -> 3.07 us  [the longest x8 2.81 us: gather_stage(): jnp.stack([value] + [shift_stage(value, stage, k) for k in range(1, stage...]
    dot_general x2 -> x4, matrix products: 11.1 us -> 12.6 us  [the longest x1 7.26 us: dense_shards(): jnp.dot(activated, jnp.concatenate(downs, axis=1), preferred_element_type...]
  transfers between devices with their start and end apart: 21 -> 21, of which waited for: 16 -> 15; matrix products, arithmetic and copies ran while one was open for 7% -> 12% of each run, Pallas kernels for 0% -> 0%
where the time goes in v3:
time: 169 us
  waiting for transfers between devices  94.6 us (56%)
  starting transfers between devices  35.5 us (21%)
  matrix products  17.5 us (10%)
  local copies, waits for them, and re-layouts  11.9 us (7%)
  other arithmetic  8.88 us (5%)
    ppermute x18, waiting for transfers between devices, shift_stage(): return lax.ppermute(value, axis, perm)  82.2 us
    ppermute x18, starting transfers between devices, shift_stage(): return lax.ppermute(value, axis, perm)  29.4 us
    ppermute x3, waiting for transfers between devices, dense_shards(): pieces = tuple((lax.ppermute(piece, 'group', perm) for piece in pieces))  12.5 us
    dot_general x1, matrix products, dense_shards(): jnp.dot(activated, jnp.concatenate(downs, axis=1), preferred_element_type...  7.26 us
    ppermute x3, starting transfers between devices, dense_shards(): pieces = tuple((lax.ppermute(piece, 'group', perm) for piece in pieces))  6.08 us
    add x2, other arithmetic, scatter_tree(): total = total + arrived.astype(jnp.float32)  3.6 us
  transfers between devices with their start and end apart: 21, of which 15 were waited for; matrix products, arithmetic and copies ran while one was open for 12% of the time, Pallas kernels for 0%

profile of v3, /device:TPU:0, one launch (start us, length us, event | category | flops | bytes accessed | tf_op | source)
XLA Modules:
  0.0 168.8 jit_solution(9520506937119837006)
XLA Ops:
  0.0 2.3 %dynamic-slice_bitcast_fusion.3 = bf16[1024,384]{1,0:T(8,128)(2,1)} fusion(bf16[1,1024,768]{2,1,0:T(8,128)(2,1)} %param.21, s32[]{:T(128)S(6)} %select_n.37), kind=kLoop, calls=%fused_computation.37 | loop fusion | bytes 1572868 | tf_op jit(solution)/shard_map/dynamic_slice | solution.py:151
  2.3 3.0 %collective-permute-start.10 = (bf16[1024,384]{1,0:T(8,128)(2,1)}, bf16[1024,384]{1,0:T(8,128)(2,1)}, u32[]{:S(2)}, u32[]{:S(2)}) collective-permute-start(bf16[1024,384]{1,0:T(8,128)(2,1)} %dynamic-slice_bitcast_fusion.3), channel_id=1, source_target_pairs={{0,16},{16,0},{1,17},{17,1},{2,18},{18,2},{3,19},{19,3},{4,20},{20... | collective-permute-start | bytes 2359304 | tf_op jit(solution)/shard_map/ppermute | solution.py:157
  5.3 0.9 reshape.153
  6.3 0.5 copy.37
  6.8 1.2 pad_maximum_fusion.3
  8.0 1.3 copy.39
  9.5 3.0 %fusion.65 = (f32[8,2,3,16]{3,2,1,0:T(4,128)S(1)}, f32[8,2,3,16,387]{4,3,2,1,0:T(8,128)}) fusion(bf16[8,387,2,64,1]{1,3,4,2,0:T(8,128)(2,1)} %bitcast.93, pred[8,3,387]{2,1,0:T(4,128)(4,1)S(1)} %broadcast_or_fusion, bf16[3,8,2,16,64]{4,3,2,1,0:T(8,128)(2,1)} %reshape.153), kind=kOutput, calls=%fused_computation.90 | convolution fusion | flops 39232896 | bytes 2092104 | tf_op jit(solution)/shard_map/sub | solution.py:271
  12.5 1.9 %convolution_bitcast_fusion = f32[3,8,2,16,64]{4,3,0,2,1:T(8,128)S(1)} fusion(bf16[8,387,2,64,1]{1,3,4,2,0:T(8,128)(2,1)S(1)} %bitcast.92, f32[8,2,3,16,387]{4,3,2,1,0:T(8,128)} %get-tuple-element.31, f32[8,2,3,16]{3,2,1,0:T(4,128)S(1)} %get-tuple-element.30), kind=kOutput, calls=%fused_computation.25 | convolution fusion | flops 38638080 | bytes 2181120 | tf_op jit(solution)/shard_map/bktgj,bjkd->tbkgd/dot_general | solution.py:273
  14.7 10.4 %collective-permute-done.6 = bf16[24,2048]{1,0:T(8,128)(2,1)S(1)} collective-permute-done((bf16[24,2048]{1,0:T(8,128)(2,1)S(1)}, bf16[24,2048]{1,0:T(8,128)(2,1)S(1)}, u32[]{:S(2)}, u32[]{:S(2)}) %collective-permute-start.6) | collective-permute-done | bytes 98336 | tf_op jit(solution)/shard_map/ppermute | solution.py:227
  25.2 2.9 %collective-permute-start.8 = (bf16[2,24,2048]{2,1,0:T(8,128)(2,1)S(1)}, bf16[2,24,2048]{2,1,0:T(8,128)(2,1)S(1)}, u32[]{:S(2)}, u32[]{:S(2)}) collective-permute-start(bf16[2,24,2048]{2,1,0:T(8,128)(2,1)S(1)} %get-tuple-element.23), channel_id=1, source_target_pairs={{0,8},{1,9},{2,10},{3,11},{4,12},{5,13},{6,14},{7,15},{8,0},{9,1},... | collective-permute-start | bytes 589832 | tf_op jit(solution)/shard_map/ppermute | solution.py:227
  28.0 1.6 collective-permute-start.7
  29.6 2.2 %collective-permute-start.9 = (bf16[2,24,2048]{2,1,0:T(8,128)(2,1)S(1)}, bf16[2,24,2048]{2,1,0:T(8,128)(2,1)S(1)}, u32[]{:S(2)}, u32[]{:S(2)}) collective-permute-start(bf16[2,24,2048]{2,1,0:T(8,128)(2,1)S(1)} %get-tuple-element.23), channel_id=1, source_target_pairs={{0,12},{1,13},{2,14},{3,15},{4,0},{5,1},{6,2},{7,3},{8,4},{9,5},{1... | collective-permute-start | bytes 589832 | tf_op jit(solution)/shard_map/ppermute | solution.py:227
  31.9 10.0 %collective-permute-done.8 = bf16[2,24,2048]{2,1,0:T(8,128)(2,1)S(1)} collective-permute-done((bf16[2,24,2048]{2,1,0:T(8,128)(2,1)S(1)}, bf16[2,24,2048]{2,1,0:T(8,128)(2,1)S(1)}, u32[]{:S(2)}, u32[]{:S(2)}) %collective-permute-start.8) | collective-permute-done | bytes 196640 | tf_op jit(solution)/shard_map/ppermute | solution.py:227
  42.3 1.6 collective-permute-start.11
  44.0 1.6 collective-permute-start.12
  45.6 13.7 %collective-permute-done.11 = bf16[4,2,24,2048]{3,2,1,0:T(8,128)(2,1)S(1)} collective-permute-done((bf16[4,2,24,2048]{3,2,1,0:T(8,128)(2,1)S(1)}, bf16[4,2,24,2048]{3,2,1,0:T(8,128)(2,1)S(1)}, u32[]{:S(2)}, u32[]{:S(2)}) %collective-permute-start.11) | collective-permute-done | bytes 786464 | tf_op jit(solution)/shard_map/ppermute | solution.py:227
  59.4 1.2 collective-permute-done.12
  60.8 1.6 collective-permute-start
  62.4 2.2 %collective-permute-done = f32[24,16]{1,0:T(8,128)S(1)} collective-permute-done((f32[24,16]{1,0:T(8,128)S(1)}, f32[24,16]{1,0:T(8,128)S(1)}, u32[]{:S(2)}, u32[]{:S(2)}) %collective-permute-start) | collective-permute-done | bytes 1568 | tf_op jit(solution)/shard_map/ppermute | solution.py:227
  64.6 7.8 %collective-permute-start.2 = (f32[2,24,16]{2,1,0:T(8,128)S(1)}, f32[2,24,16]{2,1,0:T(8,128)S(1)}, u32[]{:S(2)}, u32[]{:S(2)}) collective-permute-start(f32[2,24,16]{2,1,0:T(8,128)S(1)} %get-tuple-element.29), channel_id=1, source_target_pairs={{0,8},{1,9},{2,10},{3,11},{4,12},{5,13},{6,14},{7,15},{8,0},{9,1},... | collective-permute-start | bytes 9224 | tf_op jit(solution)/shard_map/ppermute | solution.py:227
  72.4 3.8 %collective-permute-start.3 = (f32[2,24,16]{2,1,0:T(8,128)S(1)}, f32[2,24,16]{2,1,0:T(8,128)S(1)}, u32[]{:S(2)}, u32[]{:S(2)}) collective-permute-start(f32[2,24,16]{2,1,0:T(8,128)S(1)} %get-tuple-element.29), channel_id=1, source_target_pairs={{0,12},{1,13},{2,14},{3,15},{4,0},{5,1},{6,2},{7,3},{8,4},{9,5},{1... | collective-permute-start | bytes 9224 | tf_op jit(solution)/shard_map/ppermute | solution.py:227
  76.2 1.8 %collective-permute-done.1 = f32[2,24,16]{2,1,0:T(8,128)S(1)} collective-permute-done((f32[2,24,16]{2,1,0:T(8,128)S(1)}, f32[2,24,16]{2,1,0:T(8,128)S(1)}, u32[]{:S(2)}, u32[]{:S(2)}) %collective-permute-start.1) | collective-permute-done | bytes 3104 | tf_op jit(solution)/shard_map/ppermute | solution.py:227
  78.0 0.9 collective-permute-start.4
  78.9 3.8 %collective-permute-done.4 = f32[4,2,24,16]{3,2,1,0:T(8,128)S(1)} collective-permute-done((f32[4,2,24,16]{3,2,1,0:T(8,128)S(1)}, f32[4,2,24,16]{3,2,1,0:T(8,128)S(1)}, u32[]{:S(2)}, u32[]{:S(2)}) %collective-permute-start.4) | collective-permute-done | bytes 12320 | tf_op jit(solution)/shard_map/ppermute | solution.py:227
  82.7 0.7 fusion.60
  83.4 2.6 %dynamic-slice_bitcast_fusion.1 = (bf16[384,1024]{1,0:T(8,128)(2,1)}, bf16[384,1024]{1,0:T(8,128)(2,1)}) fusion(bf16[1,768,1024]{2,1,0:T(8,128)(2,1)} %param.23, s32[]{:T(128)S(6)} %select_n.39, s32[]{:T(128)S(6)} %select_n.37), kind=kLoop, calls=%fused_computation.33 | loop fusion | bytes 3145736 | tf_op jit(solution)/shard_map/dynamic_slice | solution.py:153
  86.1 1.5 collective-permute-start.14
  88.0 1.8 %pad_maximum_fusion = bf16[2,2,4,2,24,2048]{5,4,3,2,1,0:T(8,128)(2,1)S(1)} fusion(bf16[1,2,4,2,24,2048]{5,4,3,2,1,0:T(8,128)(2,1)} %bitcast.34, bf16[1,2,4,2,24,2048]{5,4,3,2,1,0:T(8,128)(2,1)S(1)} %bitcast.89), kind=kLoop, calls=%fused_computation.4 | loop fusion | flops 1572864 | bytes 6291456 | tf_op jit(solution)/shard_map/stack | solution.py:231
  89.8 2.1 %fusion.6 = f32[768,384]{1,0:T(8,128)} fusion(bf16[1024,384]{1,0:T(8,128)(2,1)S(1)} %copy-done.15, bf16[768,2048]{1,0:T(8,128)(2,1)S(1)} %bitcast.85, s32[]{:T(128)S(6)} %select_n.40), kind=kOutput, calls=%fused_computation.15 | convolution fusion | flops 603979776 | bytes 3538948 | tf_op jit(solution)/shard_map/dot_general | solution.py:188
  91.9 2.2 %fusion.8 = f32[768,384]{1,0:T(8,128)S(1)} fusion(bf16[1024,384]{1,0:T(8,128)(2,1)} %collective-permute-done.10, bf16[768,2048]{1,0:T(8,128)(2,1)S(1)} %bitcast.86, s32[]{:T(128)S(6)} %select_n.40), kind=kOutput, calls=%fused_computation.17 | convolution fusion | flops 603979776 | bytes 3538948 | tf_op jit(solution)/shard_map/dot_general | solution.py:187
  94.1 1.0 fusion.14
  95.1 11.2 %collective-permute-done.14 = bf16[384,1024]{1,0:T(8,128)(2,1)} collective-permute-done((bf16[384,1024]{1,0:T(8,128)(2,1)}, bf16[384,1024]{1,0:T(8,128)(2,1)}, u32[]{:S(2)}, u32[]{:S(2)}) %collective-permute-start.14) | collective-permute-done | bytes 786464 | tf_op jit(solution)/shard_map/ppermute | solution.py:157
  106.4 7.3 %convolution_multiply_fusion = f32[768,2048]{1,0:T(8,128)} fusion(f32[768]{0:T(1024)S(1)} %dynamic-slice_reduce_fusion, bf16[384,1024]{1,0:T(8,128)(2,1)} %collective-permute-done.14, bf16[384,1024]{1,0:T(8,128)(2,1)S(1)} %copy-done.6, f32[768,384]{1,0:T(8,128)S(1)} %fusion.14, f32[768,384]{1,0:T(8,128)} %fusion.6, bf16[768,2048]{1,0:T(8,128)(2,1)} %bitcast.88, ...), kind=kOutput, calls=%fused_computation.1 | convolution fusion | flops 1818722304 | bytes 12587016 | tf_op jit(solution)/shard_map/dot_general | solution.py:191
  113.6 2.1 %slice.91 = bf16[384,2048]{1,0:T(8,128)(2,1)S(1)} slice(f32[768,2048]{1,0:T(8,128)} %convolution_multiply_fusion), slice={[384:768], [0:2048]} | slice | bytes 3145728 | tf_op jit(solution)/shard_map/slice | solution.py:245
  115.8 3.4 %collective-permute-done.15 = bf16[384,2048]{1,0:T(8,128)(2,1)S(1)} collective-permute-done((bf16[384,2048]{1,0:T(8,128)(2,1)S(1)}, bf16[384,2048]{1,0:T(8,128)(2,1)S(1)}, u32[]{:S(2)}, u32[]{:S(2)}) %collective-permute-start.15) | collective-permute-done | bytes 1572896 | tf_op jit(solution)/shard_map/ppermute | solution.py:227
  119.2 2.4 %slice_add_fusion = f32[384,2048]{1,0:T(8,128)S(1)} fusion(f32[768,2048]{1,0:T(8,128)} %convolution_multiply_fusion, bf16[384,2048]{1,0:T(8,128)(2,1)S(1)} %collective-permute-done.15), kind=kLoop, calls=%fused_computation.3 | loop fusion | flops 1572864 | bytes 7864320 | tf_op jit(solution)/shard_map/add | solution.py:246
  121.7 0.9 collective-permute-start.16
  122.6 18.8 %collective-permute-done.16 = bf16[192,2048]{1,0:T(8,128)(2,1)S(1)} collective-permute-done((bf16[192,2048]{1,0:T(8,128)(2,1)S(1)}, bf16[192,2048]{1,0:T(8,128)(2,1)S(1)}, u32[]{:S(2)}, u32[]{:S(2)}) %collective-permute-start.16) | collective-permute-done | bytes 786464 | tf_op jit(solution)/shard_map/ppermute | solution.py:227
  141.6 0.7 fusion.64
  142.4 3.8 %collective-permute-start.17 = (bf16[48,2048]{1,0:T(8,128)(2,1)}, bf16[48,2048]{1,0:T(8,128)(2,1)}, u32[]{:S(2)}, u32[]{:S(2)}) collective-permute-start(bf16[48,2048]{1,0:T(8,128)(2,1)} %get-tuple-element.17), channel_id=1, source_target_pairs={{0,12},{1,13},{2,14},{3,15},{4,0},{5,1},{6,2},{7,3},{8,4},{9,5},{1... | collective-permute-start | bytes 589832 | tf_op jit(solution)/shard_map/ppermute | solution.py:227
  146.2 0.6 collective-permute-start.18
  146.7 5.1 %collective-permute-done.17 = bf16[48,2048]{1,0:T(8,128)(2,1)} collective-permute-done((bf16[48,2048]{1,0:T(8,128)(2,1)}, bf16[48,2048]{1,0:T(8,128)(2,1)}, u32[]{:S(2)}, u32[]{:S(2)}) %collective-permute-start.17) | collective-permute-done | bytes 196640 | tf_op jit(solution)/shard_map/ppermute | solution.py:227
  151.8 4.4 %collective-permute-done.19 = bf16[48,2048]{1,0:T(8,128)(2,1)} collective-permute-done((bf16[48,2048]{1,0:T(8,128)(2,1)S(1)}, bf16[48,2048]{1,0:T(8,128)(2,1)}, u32[]{:S(2)}, u32[]{:S(2)}) %collective-permute-start.19) | collective-permute-done | bytes 196640 | tf_op jit(solution)/shard_map/ppermute | solution.py:227
  156.3 5.2 %collective-permute-done.18 = bf16[48,2048]{1,0:T(8,128)(2,1)} collective-permute-done((bf16[48,2048]{1,0:T(8,128)(2,1)S(1)}, bf16[48,2048]{1,0:T(8,128)(2,1)}, u32[]{:S(2)}, u32[]{:S(2)}) %collective-permute-start.18) | collective-permute-done | bytes 196640 | tf_op jit(solution)/shard_map/ppermute | solution.py:227
  161.4 1.2 fusion.35
  163.4 1.6 collective-permute-start.20
  165.0 3.1 %collective-permute-done.20 = bf16[24,2048]{1,0:T(8,128)(2,1)S(1)} collective-permute-done((bf16[24,2048]{1,0:T(8,128)(2,1)S(1)}, bf16[24,2048]{1,0:T(8,128)(2,1)S(1)}, u32[]{:S(2)}, u32[]{:S(2)}) %collective-permute-start.20) | collective-permute-done | bytes 98336 | tf_op jit(solution)/shard_map/ppermute | solution.py:227
  168.1 0.7 fusion.42
  (72 shorter events, 2.9 us)
Async XLA Ops:
  0.0 43.9 %copy-start = (bf16[1,1024,768]{2,1,0:T(8,128)(2,1)S(1)}, bf16[1,1024,768]{2,1,0:T(8,128)(2,1)}, u32[]{:S(2)}) copy-start(bf16[1,1024,768]{2,1,0:T(8,128)(2,1)} %param.22) | copy-start | bytes 4718596
  0.0 5.3 %copy-start.11 = (bf16[3,8,128]{2,1,0:T(8,128)(2,1)S(1)}, bf16[3,8,128]{2,1,0:T(8,128)(2,1)}, u32[]{:S(2)}) copy-start(bf16[3,8,128]{2,1,0:T(8,128)(2,1)} %param.14) | copy-start | bytes 18436
  0.0 5.3 %copy-start.12 = (bf16[3,8,128]{2,1,0:T(8,128)(2,1)S(1)}, bf16[3,8,128]{2,1,0:T(8,128)(2,1)}, u32[]{:S(2)}) copy-start(bf16[3,8,128]{2,1,0:T(8,128)(2,1)} %param.15) | copy-start | bytes 18436
  0.0 5.3 %copy-start.7 = (bf16[3,8,2048]{2,1,0:T(8,128)(2,1)S(1)}, bf16[3,8,2048]{2,1,0:T(8,128)(2,1)}, u32[]{:S(2)}) copy-start(bf16[3,8,2048]{2,1,0:T(8,128)(2,1)} %param.13) | copy-start | bytes 294916
  0.0 6.2 %copy-start.5 = (bf16[8,384,128]{2,1,0:T(8,128)(2,1)S(1)}, bf16[8,384,128]{2,1,0:T(8,128)(2,1)}, u32[]{:S(2)}) copy-start(bf16[8,384,128]{2,1,0:T(8,128)(2,1)} %param.17) | copy-start | bytes 2359300
  2.3 40.0 %collective-permute-start.10 = (bf16[1024,384]{1,0:T(8,128)(2,1)}, bf16[1024,384]{1,0:T(8,128)(2,1)}, u32[]{:S(2)}, u32[]{:S(2)}) collective-permute-start(bf16[1024,384]{1,0:T(8,128)(2,1)} %dynamic-slice_bitcast_fusion.3), channel_id=1, source_target_pairs={{0,16},{16,0},{1,17},{17,1},{2,18},{18,2},{3,19},{19,3},{4,20},{20... | collective-permute-start | bytes 2359304 | tf_op jit(solution)/shard_map/ppermute | solution.py:157
  6.8 2.5 %copy-start.13 = (s32[8]{0:T(128)S(1)}, s32[8]{0:T(128)}, u32[]{:S(2)}) copy-start(s32[8]{0:T(128)} %param.18) | copy-start | bytes 100
  12.5 2.1 %copy-start.8 = (bf16[3,8,2048]{2,1,0:T(8,128)(2,1)S(1)}, bf16[3,8,2048]{2,1,0:T(8,128)(2,1)}, u32[]{:S(2)}) copy-start(bf16[3,8,2048]{2,1,0:T(8,128)(2,1)} %param.12) | copy-start | bytes 294916
  14.6 27.6 %copy-start.3 = (bf16[3,8,2048]{2,1,0:T(8,128)(2,1)}, bf16[3,8,2048]{2,1,0:T(8,128)(2,1)S(1)}, u32[]{:S(2)}) copy-start(bf16[3,8,2048]{2,1,0:T(8,128)(2,1)S(1)} %add_convert_fusion) | copy-start | bytes 294916
  14.6 10.5 %collective-permute-start.6 = (bf16[24,2048]{1,0:T(8,128)(2,1)S(1)}, bf16[24,2048]{1,0:T(8,128)(2,1)S(1)}, u32[]{:S(2)}, u32[]{:S(2)}) collective-permute-start(bf16[24,2048]{1,0:T(8,128)(2,1)S(1)} %bitcast.94), channel_id=1, source_target_pairs={{0,16},{16,0},{1,17},{17,1},{2,18},{18,2},{3,19},{19,3},{4,20},{20... | collective-permute-start | bytes 294920 | tf_op jit(solution)/shard_map/ppermute | solution.py:227
  25.2 16.7 %collective-permute-start.8 = (bf16[2,24,2048]{2,1,0:T(8,128)(2,1)S(1)}, bf16[2,24,2048]{2,1,0:T(8,128)(2,1)S(1)}, u32[]{:S(2)}, u32[]{:S(2)}) collective-permute-start(bf16[2,24,2048]{2,1,0:T(8,128)(2,1)S(1)} %get-tuple-element.23), channel_id=1, source_target_pairs={{0,8},{1,9},{2,10},{3,11},{4,12},{5,13},{6,14},{7,15},{8,0},{9,1},... | collective-permute-start | bytes 589832 | tf_op jit(solution)/shard_map/ppermute | solution.py:227
  28.0 13.8 %collective-permute-start.7 = (bf16[2,24,2048]{2,1,0:T(8,128)(2,1)S(1)}, bf16[2,24,2048]{2,1,0:T(8,128)(2,1)S(1)}, u32[]{:S(2)}, u32[]{:S(2)}) collective-permute-start(bf16[2,24,2048]{2,1,0:T(8,128)(2,1)S(1)} %get-tuple-element.23), channel_id=1, source_target_pairs={{0,4},{1,5},{2,6},{3,7},{4,8},{5,9},{6,10},{7,11},{8,12},{9,13},{1... | collective-permute-start | bytes 589832 | tf_op jit(solution)/shard_map/ppermute | solution.py:227
  29.6 12.6 %collective-permute-start.9 = (bf16[2,24,2048]{2,1,0:T(8,128)(2,1)S(1)}, bf16[2,24,2048]{2,1,0:T(8,128)(2,1)S(1)}, u32[]{:S(2)}, u32[]{:S(2)}) collective-permute-start(bf16[2,24,2048]{2,1,0:T(8,128)(2,1)S(1)} %get-tuple-element.23), channel_id=1, source_target_pairs={{0,12},{1,13},{2,14},{3,15},{4,0},{5,1},{6,2},{7,3},{8,4},{9,5},{1... | collective-permute-start | bytes 589832 | tf_op jit(solution)/shard_map/ppermute | solution.py:227
  42.3 16.9 %collective-permute-start.11 = (bf16[4,2,24,2048]{3,2,1,0:T(8,128)(2,1)S(1)}, bf16[4,2,24,2048]{3,2,1,0:T(8,128)(2,1)S(1)}, u32[]{:S(2)}, u32[]{:S(2)}) collective-permute-start(bf16[4,2,24,2048]{3,2,1,0:T(8,128)(2,1)S(1)} %pad_maximum_fusion.4), channel_id=1, source_target_pairs={{0,2},{1,3},{2,0},{3,1},{4,6},{5,7},{6,4},{7,5},{8,10},{9,11},{10,... | collective-permute-start | bytes 2359304 | tf_op jit(solution)/shard_map/ppermute | solution.py:227
  44.0 16.6 %collective-permute-start.12 = (bf16[1024,384]{1,0:T(8,128)(2,1)S(1)}, bf16[1024,384]{1,0:T(8,128)(2,1)S(1)}, u32[]{:S(2)}, u32[]{:S(2)}) collective-permute-start(bf16[1024,384]{1,0:T(8,128)(2,1)S(1)} %dynamic-slice_bitcast_fusion.2), channel_id=1, source_target_pairs={{0,16},{16,0},{1,17},{17,1},{2,18},{18,2},{3,19},{19,3},{4,20},{20... | collective-permute-start | bytes 2359304 | tf_op jit(solution)/shard_map/ppermute | solution.py:157
  59.2 1.4 copy-start.9
  59.2 1.4 copy-start.10
  60.6 17.4 %copy-start.14 = (bf16[1024,384]{1,0:T(8,128)(2,1)}, bf16[1024,384]{1,0:T(8,128)(2,1)S(1)}, u32[]{:S(2)}) copy-start(bf16[1024,384]{1,0:T(8,128)(2,1)S(1)} %collective-permute-done.12) | copy-start | bytes 2359300
  60.6 27.3 %collective-permute-start.13 = (bf16[2,4,2,24,2048]{4,3,2,1,0:T(8,128)(2,1)S(1)}, bf16[2,4,2,24,2048]{4,3,2,1,0:T(8,128)(2,1)}, u32[]{:S(2)}, u32[]{:S(2)}) collective-permute-start(bf16[2,4,2,24,2048]{4,3,2,1,0:T(8,128)(2,1)S(1)} %pad_maximum_fusion.1), channel_id=1, source_target_pairs={{0,1},{1,0},{2,3},{3,2},{4,5},{5,4},{6,7},{7,6},{8,9},{9,8},{10,11... | collective-permute-start | bytes 4718600 | tf_op jit(solution)/shard_map/ppermute | solution.py:227
  60.8 3.8 %collective-permute-start = (f32[24,16]{1,0:T(8,128)S(1)}, f32[24,16]{1,0:T(8,128)S(1)}, u32[]{:S(2)}, u32[]{:S(2)}) collective-permute-start(f32[24,16]{1,0:T(8,128)S(1)} %bitcast.103), channel_id=1, source_target_pairs={{0,16},{16,0},{1,17},{17,1},{2,18},{18,2},{3,19},{19,3},{4,20},{20... | collective-permute-start | bytes 4616 | tf_op jit(solution)/shard_map/ppermute | solution.py:227
  64.6 11.7 %collective-permute-start.2 = (f32[2,24,16]{2,1,0:T(8,128)S(1)}, f32[2,24,16]{2,1,0:T(8,128)S(1)}, u32[]{:S(2)}, u32[]{:S(2)}) collective-permute-start(f32[2,24,16]{2,1,0:T(8,128)S(1)} %get-tuple-element.29), channel_id=1, source_target_pairs={{0,8},{1,9},{2,10},{3,11},{4,12},{5,13},{6,14},{7,15},{8,0},{9,1},... | collective-permute-start | bytes 9224 | tf_op jit(solution)/shard_map/ppermute | solution.py:227
  72.4 5.6 %collective-permute-start.1 = (f32[2,24,16]{2,1,0:T(8,128)S(1)}, f32[2,24,16]{2,1,0:T(8,128)S(1)}, u32[]{:S(2)}, u32[]{:S(2)}) collective-permute-start(f32[2,24,16]{2,1,0:T(8,128)S(1)} %get-tuple-element.29), channel_id=1, source_target_pairs={{0,4},{1,5},{2,6},{3,7},{4,8},{5,9},{6,10},{7,11},{8,12},{9,13},{1... | collective-permute-start | bytes 9224 | tf_op jit(solution)/shard_map/ppermute | solution.py:227
  72.4 5.6 %collective-permute-start.3 = (f32[2,24,16]{2,1,0:T(8,128)S(1)}, f32[2,24,16]{2,1,0:T(8,128)S(1)}, u32[]{:S(2)}, u32[]{:S(2)}) collective-permute-start(f32[2,24,16]{2,1,0:T(8,128)S(1)} %get-tuple-element.29), channel_id=1, source_target_pairs={{0,12},{1,13},{2,14},{3,15},{4,0},{5,1},{6,2},{7,3},{8,4},{9,5},{1... | collective-permute-start | bytes 9224 | tf_op jit(solution)/shard_map/ppermute | solution.py:227
  78.0 4.7 %collective-permute-start.4 = (f32[4,2,24,16]{3,2,1,0:T(8,128)S(1)}, f32[4,2,24,16]{3,2,1,0:T(8,128)S(1)}, u32[]{:S(2)}, u32[]{:S(2)}) collective-permute-start(f32[4,2,24,16]{3,2,1,0:T(8,128)S(1)} %get-tuple-element.27), channel_id=1, source_target_pairs={{0,2},{1,3},{2,0},{3,1},{4,6},{5,7},{6,4},{7,5},{8,10},{9,11},{10,... | collective-permute-start | bytes 36872 | tf_op jit(solution)/shard_map/ppermute | solution.py:227
  83.4 4.2 %collective-permute-start.5 = (f32[2,4,2,24,16]{4,3,2,1,0:T(8,128)}, f32[2,4,2,24,16]{4,3,2,1,0:T(8,128)S(1)}, u32[]{:S(2)}, u32[]{:S(2)}) collective-permute-start(f32[2,4,2,24,16]{4,3,2,1,0:T(8,128)} %get-tuple-element.25), channel_id=1, source_target_pairs={{0,1},{1,0},{2,3},{3,2},{4,5},{5,4},{6,7},{7,6},{8,9},{9,8},{10,11... | collective-permute-start | bytes 73736 | tf_op jit(solution)/shard_map/ppermute | solution.py:227
  86.1 20.3 %collective-permute-start.14 = (bf16[384,1024]{1,0:T(8,128)(2,1)}, bf16[384,1024]{1,0:T(8,128)(2,1)}, u32[]{:S(2)}, u32[]{:S(2)}) collective-permute-start(bf16[384,1024]{1,0:T(8,128)(2,1)} %get-tuple-element.16), channel_id=1, source_target_pairs={{0,16},{16,0},{1,17},{17,1},{2,18},{18,2},{3,19},{19,3},{4,20},{20... | collective-permute-start | bytes 2359304 | tf_op jit(solution)/shard_map/ppermute | solution.py:157
  88.0 1.8 %copy-start.15 = (bf16[1024,384]{1,0:T(8,128)(2,1)S(1)}, bf16[1024,384]{1,0:T(8,128)(2,1)}, u32[]{:S(2)}) copy-start(bf16[1024,384]{1,0:T(8,128)(2,1)} %copy-done.14) | copy-start | bytes 2359300
  89.7 4.3 %copy-start.1 = (bf16[2,2,4,2,24,2048]{5,4,3,2,1,0:T(8,128)(2,1)}, bf16[2,2,4,2,24,2048]{5,4,3,2,1,0:T(8,128)(2,1)S(1)}, u32[]{:S(2)}) copy-start(bf16[2,2,4,2,24,2048]{5,4,3,2,1,0:T(8,128)(2,1)S(1)} %pad_maximum_fusion) | copy-start | bytes 9437188
  91.9 2.2 %copy-start.2 = (bf16[1,1024,768]{2,1,0:T(8,128)(2,1)S(1)}, bf16[1,1024,768]{2,1,0:T(8,128)(2,1)}, u32[]{:S(2)}) copy-start(bf16[1,1024,768]{2,1,0:T(8,128)(2,1)} %param.21) | copy-start | bytes 4718596
  94.1 12.3 %copy-start.6 = (bf16[384,1024]{1,0:T(8,128)(2,1)S(1)}, bf16[384,1024]{1,0:T(8,128)(2,1)}, u32[]{:S(2)}) copy-start(bf16[384,1024]{1,0:T(8,128)(2,1)} %get-tuple-element.15) | copy-start | bytes 2359300
  115.7 3.5 %collective-permute-start.15 = (bf16[384,2048]{1,0:T(8,128)(2,1)S(1)}, bf16[384,2048]{1,0:T(8,128)(2,1)S(1)}, u32[]{:S(2)}, u32[]{:S(2)}) collective-permute-start(bf16[384,2048]{1,0:T(8,128)(2,1)S(1)} %slice.91), channel_id=1, source_target_pairs={{0,1},{1,0},{2,3},{3,2},{4,5},{5,4},{6,7},{7,6},{8,9},{9,8},{10,11... | collective-permute-start | bytes 4718600 | tf_op jit(solution)/shard_map/ppermute | solution.py:227
  121.7 19.6 %collective-permute-start.16 = (bf16[192,2048]{1,0:T(8,128)(2,1)S(1)}, bf16[192,2048]{1,0:T(8,128)(2,1)S(1)}, u32[]{:S(2)}, u32[]{:S(2)}) collective-permute-start(bf16[192,2048]{1,0:T(8,128)(2,1)S(1)} %slice.92), channel_id=1, source_target_pairs={{0,2},{1,3},{2,0},{3,1},{4,6},{5,7},{6,4},{7,5},{8,10},{9,11},{10,... | collective-permute-start | bytes 2359304 | tf_op jit(solution)/shard_map/ppermute | solution.py:227
  142.4 9.5 %collective-permute-start.17 = (bf16[48,2048]{1,0:T(8,128)(2,1)}, bf16[48,2048]{1,0:T(8,128)(2,1)}, u32[]{:S(2)}, u32[]{:S(2)}) collective-permute-start(bf16[48,2048]{1,0:T(8,128)(2,1)} %get-tuple-element.17), channel_id=1, source_target_pairs={{0,12},{1,13},{2,14},{3,15},{4,0},{5,1},{6,2},{7,3},{8,4},{9,5},{1... | collective-permute-start | bytes 589832 | tf_op jit(solution)/shard_map/ppermute | solution.py:227
  146.2 10.1 %collective-permute-start.19 = (bf16[48,2048]{1,0:T(8,128)(2,1)S(1)}, bf16[48,2048]{1,0:T(8,128)(2,1)}, u32[]{:S(2)}, u32[]{:S(2)}) collective-permute-start(bf16[48,2048]{1,0:T(8,128)(2,1)S(1)} %get-tuple-element.18), channel_id=1, source_target_pairs={{0,4},{1,5},{2,6},{3,7},{4,8},{5,9},{6,10},{7,11},{8,12},{9,13},{1... | collective-permute-start | bytes 589832 | tf_op jit(solution)/shard_map/ppermute | solution.py:227
  146.2 15.3 %collective-permute-start.18 = (bf16[48,2048]{1,0:T(8,128)(2,1)S(1)}, bf16[48,2048]{1,0:T(8,128)(2,1)}, u32[]{:S(2)}, u32[]{:S(2)}) collective-permute-start(bf16[48,2048]{1,0:T(8,128)(2,1)S(1)} %get-tuple-element.19), channel_id=1, source_target_pairs={{0,8},{1,9},{2,10},{3,11},{4,12},{5,13},{6,14},{7,15},{8,0},{9,1},... | collective-permute-start | bytes 589832 | tf_op jit(solution)/shard_map/ppermute | solution.py:227
  162.6 5.5 %copy-start.4 = (bf16[3,8,2048]{2,1,0:T(8,128)(2,1)S(1)}, bf16[3,8,2048]{2,1,0:T(8,128)(2,1)}, u32[]{:S(2)}) copy-start(bf16[3,8,2048]{2,1,0:T(8,128)(2,1)} %copy-done.3) | copy-start | bytes 294916
  163.4 4.7 %collective-permute-start.20 = (bf16[24,2048]{1,0:T(8,128)(2,1)S(1)}, bf16[24,2048]{1,0:T(8,128)(2,1)S(1)}, u32[]{:S(2)}, u32[]{:S(2)}) collective-permute-start(bf16[24,2048]{1,0:T(8,128)(2,1)S(1)} %fusion.40), channel_id=1, source_target_pairs={{0,16},{16,0},{1,17},{17,1},{2,18},{18,2},{3,19},{19,3},{4,20},{20... | collective-permute-start | bytes 294920 | tf_op jit(solution)/shard_map/ppermute | solution.py:227

commit v4 on v3

--- a/solution.py
+++ b/solution.py
@@ -174,8 +174,10 @@
     arriving = [piece for k in range(1, groups) for piece in pairs[k][1]]
     tokens = flat
     for number, stage in enumerate(stages):
-        if number >= 2 and number - 2 < len(arriving):
-            tokens, arriving[number - 2] = lax.optimization_barrier((tokens, arriving[number - 2]))
+        if number == 2:
+            tokens, arriving[:2] = lax.optimization_barrier((tokens, arriving[:2]))
+        elif number == 3:
+            tokens, arriving[2:] = lax.optimization_barrier((tokens, arriving[2:]))
         tokens = gather_stage(tokens, stage)
     tokens = tokens.reshape(-1, width)
     gate_val, up_val, downs = 0.0, 0.0, []

time: 169 us -> 177 us (1.047)
  other arithmetic: 8.88 us -> 11.6 us
  local copies, waits for them, and re-layouts: 11.9 us -> 13.7 us
    ppermute x18, waiting for transfers between devices: 82.2 us -> 94.6 us  [shift_stage(): return lax.ppermute(value, axis, perm)]
    ppermute x3, waiting for transfers between devices: 12.5 us -> 1.18 us  [dense_shards(): pieces = tuple((lax.ppermute(piece, 'group', perm) for piece in pieces))]
    unnamed x35 -> x37, local copies, waits for them, and re-layouts: 0.15 us -> 2.56 us
  transfers between devices with their start and end apart: 21 -> 21, of which waited for: 15 -> 15; matrix products, arithmetic and copies ran while one was open for 12% -> 10% of each run, Pallas kernels for 0% -> 0%
where the time goes in v4:
time: 177 us; the launch traced here: 176 us
  waiting for transfers between devices  95.8 us (54%)
  starting transfers between devices  35.5 us (20%)
  matrix products  19.1 us (11%)
  local copies, waits for them, and re-layouts  13.7 us (8%)
  other arithmetic  11.6 us (7%)
    ppermute x18, waiting for transfers between devices, shift_stage(): return lax.ppermute(value, axis, perm)  94.6 us
    ppermute x18, starting transfers between devices, shift_stage(): return lax.ppermute(value, axis, perm)  31 us
    dot_general x1, matrix products, dense_shards(): jnp.dot(activated, jnp.concatenate(downs, axis=1), preferred_element_type...  7.27 us
    ppermute x3, starting transfers between devices, dense_shards(): pieces = tuple((lax.ppermute(piece, 'group', perm) for piece in pieces))  4.49 us
    another operation x8, other arithmetic, gather_stage(): jnp.stack([value] + [shift_stage(value, stage, k) for k in range(1, stage...  4.37 us
    dot_general x1, matrix products, dense_shards(): jnp.dot(share, pieces[1], preferred_element_type=jnp.float32)  3.73 us
    add x2, other arithmetic, scatter_tree(): total = total + arrived.astype(jnp.float32)  3.6 us
  transfers between devices with their start and end apart: 21, of which 15 were waited for; matrix products, arithmetic and copies ran while one was open for 10% of the time, Pallas kernels for 0%

profile of v4, /device:TPU:0, one launch (start us, length us, event | category | flops | bytes accessed | tf_op | source)
XLA Modules:
  0.0 176.2 jit_solution(7713591905980060756)
XLA Ops:
  0.0 1.4 copy-done
  1.4 1.0 dynamic-slice_bitcast_fusion.2
  2.4 3.0 %collective-permute-start.11 = (bf16[1024,384]{1,0:T(8,128)(2,1)}, bf16[1024,384]{1,0:T(8,128)(2,1)}, u32[]{:S(2)}, u32[]{:S(2)}) collective-permute-start(bf16[1024,384]{1,0:T(8,128)(2,1)} %dynamic-slice_bitcast_fusion.2), channel_id=1, source_target_pairs={{0,16},{16,0},{1,17},{17,1},{2,18},{18,2},{3,19},{19,3},{4,20},{20... | collective-permute-start | bytes 2359304 | tf_op jit(solution)/shard_map/ppermute | solution.py:157
  5.4 1.0 dynamic-slice_bitcast_fusion.3
  6.4 0.9 reshape.153
  7.3 1.2 pad_maximum_fusion.2
  9.0 1.2 pad_maximum_fusion.3
  10.2 1.3 copy.39
  11.7 3.0 %fusion.65 = (f32[8,2,3,16]{3,2,1,0:T(4,128)S(1)}, f32[8,2,3,16,387]{4,3,2,1,0:T(8,128)}) fusion(bf16[8,387,2,64,1]{1,3,4,2,0:T(8,128)(2,1)} %bitcast.93, pred[8,3,387]{2,1,0:T(4,128)(4,1)S(1)} %broadcast_or_fusion, bf16[3,8,2,16,64]{4,3,2,1,0:T(8,128)(2,1)} %reshape.153), kind=kOutput, calls=%fused_computation.90 | convolution fusion | flops 39232896 | bytes 2092104 | tf_op jit(solution)/shard_map/sub | solution.py:273
  14.7 1.9 %convolution_bitcast_fusion = f32[3,8,2,16,64]{4,3,0,2,1:T(8,128)S(1)} fusion(bf16[8,387,2,64,1]{1,3,4,2,0:T(8,128)(2,1)S(1)} %bitcast.92, f32[8,2,3,16,387]{4,3,2,1,0:T(8,128)} %get-tuple-element.33, f32[8,2,3,16]{3,2,1,0:T(4,128)S(1)} %get-tuple-element.32), kind=kOutput, calls=%fused_computation.25 | convolution fusion | flops 38638080 | bytes 2181120 | tf_op jit(solution)/shard_map/bktgj,bjkd->tbkgd/dot_general | solution.py:275
  16.9 2.1 %collective-permute-start.6 = (bf16[24,2048]{1,0:T(8,128)(2,1)S(1)}, bf16[24,2048]{1,0:T(8,128)(2,1)S(1)}, u32[]{:S(2)}, u32[]{:S(2)}) collective-permute-start(bf16[24,2048]{1,0:T(8,128)(2,1)S(1)} %bitcast.94), channel_id=1, source_target_pairs={{0,16},{16,0},{1,17},{17,1},{2,18},{18,2},{3,19},{19,3},{4,20},{20... | collective-permute-start | bytes 294920 | tf_op jit(solution)/shard_map/ppermute | solution.py:229
  19.0 23.1 %collective-permute-done.6 = bf16[24,2048]{1,0:T(8,128)(2,1)S(1)} collective-permute-done((bf16[24,2048]{1,0:T(8,128)(2,1)S(1)}, bf16[24,2048]{1,0:T(8,128)(2,1)S(1)}, u32[]{:S(2)}, u32[]{:S(2)}) %collective-permute-start.6) | collective-permute-done | bytes 98336 | tf_op jit(solution)/shard_map/ppermute | solution.py:229
  42.1 2.9 %collective-permute-start.8 = (bf16[2,24,2048]{2,1,0:T(8,128)(2,1)S(1)}, bf16[2,24,2048]{2,1,0:T(8,128)(2,1)S(1)}, u32[]{:S(2)}, u32[]{:S(2)}) collective-permute-start(bf16[2,24,2048]{2,1,0:T(8,128)(2,1)S(1)} %get-tuple-element.25), channel_id=1, source_target_pairs={{0,8},{1,9},{2,10},{3,11},{4,12},{5,13},{6,14},{7,15},{8,0},{9,1},... | collective-permute-start | bytes 589832 | tf_op jit(solution)/shard_map/ppermute | solution.py:229
  45.0 1.6 collective-permute-start.7
  46.6 2.2 %collective-permute-start.9 = (bf16[2,24,2048]{2,1,0:T(8,128)(2,1)S(1)}, bf16[2,24,2048]{2,1,0:T(8,128)(2,1)S(1)}, u32[]{:S(2)}, u32[]{:S(2)}) collective-permute-start(bf16[2,24,2048]{2,1,0:T(8,128)(2,1)S(1)} %get-tuple-element.25), channel_id=1, source_target_pairs={{0,12},{1,13},{2,14},{3,15},{4,0},{5,1},{6,2},{7,3},{8,4},{9,5},{1... | collective-permute-start | bytes 589832 | tf_op jit(solution)/shard_map/ppermute | solution.py:229
  48.8 10.0 %collective-permute-done.8 = bf16[2,24,2048]{2,1,0:T(8,128)(2,1)S(1)} collective-permute-done((bf16[2,24,2048]{2,1,0:T(8,128)(2,1)S(1)}, bf16[2,24,2048]{2,1,0:T(8,128)(2,1)S(1)}, u32[]{:S(2)}, u32[]{:S(2)}) %collective-permute-start.8) | collective-permute-done | bytes 196640 | tf_op jit(solution)/shard_map/ppermute | solution.py:229
  59.3 1.6 collective-permute-start.12
  60.9 2.4 %dynamic-slice_bitcast_fusion = (bf16[384,1024]{1,0:T(8,128)(2,1)}, bf16[384,1024]{1,0:T(8,128)(2,1)S(1)}) fusion(bf16[1,768,1024]{2,1,0:T(8,128)(2,1)} %param.23, s32[]{:T(128)S(6)} %select_n.39, s32[]{:T(128)S(6)} %select_n.37), kind=kLoop, calls=%fused_computation.32 | loop fusion | bytes 3145736 | tf_op jit(solution)/shard_map/dynamic_slice | solution.py:153
  63.3 1.5 collective-permute-start.13
  64.8 11.4 %collective-permute-done.12 = bf16[4,2,24,2048]{3,2,1,0:T(8,128)(2,1)S(1)} collective-permute-done((bf16[4,2,24,2048]{3,2,1,0:T(8,128)(2,1)S(1)}, bf16[4,2,24,2048]{3,2,1,0:T(8,128)(2,1)S(1)}, u32[]{:S(2)}, u32[]{:S(2)}) %collective-permute-start.12) | collective-permute-done | bytes 786464 | tf_op jit(solution)/shard_map/ppermute | solution.py:229
  76.2 0.9 copy-done.8
  77.1 1.5 pad_maximum_fusion.1
  78.7 1.2 collective-permute-done.13
  80.0 1.6 collective-permute-start
  81.6 2.2 %collective-permute-done = f32[24,16]{1,0:T(8,128)S(1)} collective-permute-done((f32[24,16]{1,0:T(8,128)S(1)}, f32[24,16]{1,0:T(8,128)S(1)}, u32[]{:S(2)}, u32[]{:S(2)}) %collective-permute-start) | collective-permute-done | bytes 1568 | tf_op jit(solution)/shard_map/ppermute | solution.py:229
  83.8 7.8 %collective-permute-start.2 = (f32[2,24,16]{2,1,0:T(8,128)S(1)}, f32[2,24,16]{2,1,0:T(8,128)S(1)}, u32[]{:S(2)}, u32[]{:S(2)}) collective-permute-start(f32[2,24,16]{2,1,0:T(8,128)S(1)} %get-tuple-element.31), channel_id=1, source_target_pairs={{0,8},{1,9},{2,10},{3,11},{4,12},{5,13},{6,14},{7,15},{8,0},{9,1},... | collective-permute-start | bytes 9224 | tf_op jit(solution)/shard_map/ppermute | solution.py:229
  91.6 3.8 %collective-permute-start.3 = (f32[2,24,16]{2,1,0:T(8,128)S(1)}, f32[2,24,16]{2,1,0:T(8,128)S(1)}, u32[]{:S(2)}, u32[]{:S(2)}) collective-permute-start(f32[2,24,16]{2,1,0:T(8,128)S(1)} %get-tuple-element.31), channel_id=1, source_target_pairs={{0,12},{1,13},{2,14},{3,15},{4,0},{5,1},{6,2},{7,3},{8,4},{9,5},{1... | collective-permute-start | bytes 9224 | tf_op jit(solution)/shard_map/ppermute | solution.py:229
  95.4 1.8 %collective-permute-done.1 = f32[2,24,16]{2,1,0:T(8,128)S(1)} collective-permute-done((f32[2,24,16]{2,1,0:T(8,128)S(1)}, f32[2,24,16]{2,1,0:T(8,128)S(1)}, u32[]{:S(2)}, u32[]{:S(2)}) %collective-permute-start.1) | collective-permute-done | bytes 3104 | tf_op jit(solution)/shard_map/ppermute | solution.py:229
  97.8 4.1 %collective-permute-done.4 = f32[4,2,24,16]{3,2,1,0:T(8,128)S(1)} collective-permute-done((f32[4,2,24,16]{3,2,1,0:T(8,128)S(1)}, f32[4,2,24,16]{3,2,1,0:T(8,128)S(1)}, u32[]{:S(2)}, u32[]{:S(2)}) %collective-permute-start.4) | collective-permute-done | bytes 12320 | tf_op jit(solution)/shard_map/ppermute | solution.py:229
  102.1 1.5 collective-permute-done.5
  103.6 1.0 pad_maximum_fusion.5
  104.9 1.7 pad_maximum_fusion
  106.6 3.7 %fusion.6 = f32[768,384]{1,0:T(8,128)} fusion(bf16[1024,384]{1,0:T(8,128)(2,1)} %collective-permute-done.11, bf16[768,2048]{1,0:T(8,128)(2,1)S(1)} %bitcast.85, s32[]{:T(128)S(6)} %select_n.40), kind=kOutput, calls=%fused_computation.15 | convolution fusion | flops 603979776 | bytes 3538948 | tf_op jit(solution)/shard_map/dot_general | solution.py:190
  110.3 2.2 %fusion.8 = f32[768,384]{1,0:T(8,128)S(1)} fusion(bf16[1024,384]{1,0:T(8,128)(2,1)} %collective-permute-done.10, bf16[768,2048]{1,0:T(8,128)(2,1)S(1)} %bitcast.86, s32[]{:T(128)S(6)} %select_n.40), kind=kOutput, calls=%fused_computation.17 | convolution fusion | flops 603979776 | bytes 3538948 | tf_op jit(solution)/shard_map/dot_general | solution.py:189
  112.6 1.0 fusion.14
  113.7 7.3 %convolution_multiply_fusion = f32[768,2048]{1,0:T(8,128)} fusion(f32[768]{0:T(1024)S(1)} %dynamic-slice_reduce_fusion, bf16[384,1024]{1,0:T(8,128)(2,1)} %copy-done.16, bf16[384,1024]{1,0:T(8,128)(2,1)S(1)} %copy-done.7, f32[768,384]{1,0:T(8,128)S(1)} %fusion.14, f32[768,384]{1,0:T(8,128)} %fusion.6, bf16[768,2048]{1,0:T(8,128)(2,1)} %bitcast.88, ...), kind=kOutput, calls=%fused_computation.1 | convolution fusion | flops 1818722304 | bytes 12587016 | tf_op jit(solution)/shard_map/dot_general | solution.py:193
  121.0 2.1 %slice.91 = bf16[384,2048]{1,0:T(8,128)(2,1)S(1)} slice(f32[768,2048]{1,0:T(8,128)} %convolution_multiply_fusion), slice={[384:768], [0:2048]} | slice | bytes 3145728 | tf_op jit(solution)/shard_map/slice | solution.py:247
  123.3 3.3 %collective-permute-done.15 = bf16[384,2048]{1,0:T(8,128)(2,1)S(1)} collective-permute-done((bf16[384,2048]{1,0:T(8,128)(2,1)S(1)}, bf16[384,2048]{1,0:T(8,128)(2,1)S(1)}, u32[]{:S(2)}, u32[]{:S(2)}) %collective-permute-start.15) | collective-permute-done | bytes 1572896 | tf_op jit(solution)/shard_map/ppermute | solution.py:229
  126.6 2.4 %slice_add_fusion = f32[384,2048]{1,0:T(8,128)S(1)} fusion(f32[768,2048]{1,0:T(8,128)} %convolution_multiply_fusion, bf16[384,2048]{1,0:T(8,128)(2,1)S(1)} %collective-permute-done.15), kind=kLoop, calls=%fused_computation.3 | loop fusion | flops 1572864 | bytes 7864320 | tf_op jit(solution)/shard_map/add | solution.py:248
  129.7 19.0 %collective-permute-done.16 = bf16[192,2048]{1,0:T(8,128)(2,1)S(1)} collective-permute-done((bf16[192,2048]{1,0:T(8,128)(2,1)S(1)}, bf16[192,2048]{1,0:T(8,128)(2,1)S(1)}, u32[]{:S(2)}, u32[]{:S(2)}) %collective-permute-start.16) | collective-permute-done | bytes 786464 | tf_op jit(solution)/shard_map/ppermute | solution.py:229
  149.0 0.7 fusion.64
  149.7 3.8 %collective-permute-start.17 = (bf16[48,2048]{1,0:T(8,128)(2,1)}, bf16[48,2048]{1,0:T(8,128)(2,1)}, u32[]{:S(2)}, u32[]{:S(2)}) collective-permute-start(bf16[48,2048]{1,0:T(8,128)(2,1)} %get-tuple-element.19), channel_id=1, source_target_pairs={{0,12},{1,13},{2,14},{3,15},{4,0},{5,1},{6,2},{7,3},{8,4},{9,5},{1... | collective-permute-start | bytes 589832 | tf_op jit(solution)/shard_map/ppermute | solution.py:229
  154.1 5.1 %collective-permute-done.17 = bf16[48,2048]{1,0:T(8,128)(2,1)} collective-permute-done((bf16[48,2048]{1,0:T(8,128)(2,1)}, bf16[48,2048]{1,0:T(8,128)(2,1)}, u32[]{:S(2)}, u32[]{:S(2)}) %collective-permute-start.17) | collective-permute-done | bytes 196640 | tf_op jit(solution)/shard_map/ppermute | solution.py:229
  159.2 4.4 %collective-permute-done.19 = bf16[48,2048]{1,0:T(8,128)(2,1)} collective-permute-done((bf16[48,2048]{1,0:T(8,128)(2,1)S(1)}, bf16[48,2048]{1,0:T(8,128)(2,1)}, u32[]{:S(2)}, u32[]{:S(2)}) %collective-permute-start.19) | collective-permute-done | bytes 196640 | tf_op jit(solution)/shard_map/ppermute | solution.py:229
  163.6 5.2 %collective-permute-done.18 = bf16[48,2048]{1,0:T(8,128)(2,1)} collective-permute-done((bf16[48,2048]{1,0:T(8,128)(2,1)S(1)}, bf16[48,2048]{1,0:T(8,128)(2,1)}, u32[]{:S(2)}, u32[]{:S(2)}) %collective-permute-start.18) | collective-permute-done | bytes 196640 | tf_op jit(solution)/shard_map/ppermute | solution.py:229
  168.8 1.2 fusion.35
  170.8 1.6 collective-permute-start.20
  172.4 3.1 %collective-permute-done.20 = bf16[24,2048]{1,0:T(8,128)(2,1)S(1)} collective-permute-done((bf16[24,2048]{1,0:T(8,128)(2,1)S(1)}, bf16[24,2048]{1,0:T(8,128)(2,1)S(1)}, u32[]{:S(2)}, u32[]{:S(2)}) %collective-permute-start.20) | collective-permute-done | bytes 98336 | tf_op jit(solution)/shard_map/ppermute | solution.py:229
  (74 shorter events, 5.9 us)
Async XLA Ops:
  0.0 1.4 copy-start
  0.0 5.4 %copy-start.3 = (bf16[1,1024,768]{2,1,0:T(8,128)(2,1)S(1)}, bf16[1,1024,768]{2,1,0:T(8,128)(2,1)}, u32[]{:S(2)}) copy-start(bf16[1,1024,768]{2,1,0:T(8,128)(2,1)} %param.21) | copy-start | bytes 4718596
  1.4 5.0 %copy-start.13 = (bf16[3,8,128]{2,1,0:T(8,128)(2,1)S(1)}, bf16[3,8,128]{2,1,0:T(8,128)(2,1)}, u32[]{:S(2)}) copy-start(bf16[3,8,128]{2,1,0:T(8,128)(2,1)} %param.14) | copy-start | bytes 18436
  1.4 5.0 %copy-start.14 = (bf16[3,8,128]{2,1,0:T(8,128)(2,1)S(1)}, bf16[3,8,128]{2,1,0:T(8,128)(2,1)}, u32[]{:S(2)}) copy-start(bf16[3,8,128]{2,1,0:T(8,128)(2,1)} %param.15) | copy-start | bytes 18436
  1.4 5.0 %copy-start.9 = (bf16[3,8,2048]{2,1,0:T(8,128)(2,1)S(1)}, bf16[3,8,2048]{2,1,0:T(8,128)(2,1)}, u32[]{:S(2)}) copy-start(bf16[3,8,2048]{2,1,0:T(8,128)(2,1)} %param.13) | copy-start | bytes 294916
  2.4 56.9 %collective-permute-start.11 = (bf16[1024,384]{1,0:T(8,128)(2,1)}, bf16[1024,384]{1,0:T(8,128)(2,1)}, u32[]{:S(2)}, u32[]{:S(2)}) collective-permute-start(bf16[1024,384]{1,0:T(8,128)(2,1)} %dynamic-slice_bitcast_fusion.2), channel_id=1, source_target_pairs={{0,16},{16,0},{1,17},{17,1},{2,18},{18,2},{3,19},{19,3},{4,20},{20... | collective-permute-start | bytes 2359304 | tf_op jit(solution)/shard_map/ppermute | solution.py:157
  6.4 53.0 %collective-permute-start.10 = (bf16[1024,384]{1,0:T(8,128)(2,1)}, bf16[1024,384]{1,0:T(8,128)(2,1)}, u32[]{:S(2)}, u32[]{:S(2)}) collective-permute-start(bf16[1024,384]{1,0:T(8,128)(2,1)} %dynamic-slice_bitcast_fusion.3), channel_id=1, source_target_pairs={{0,16},{16,0},{1,17},{17,1},{2,18},{18,2},{3,19},{19,3},{4,20},{20... | collective-permute-start | bytes 2359304 | tf_op jit(solution)/shard_map/ppermute | solution.py:157
  9.0 2.5 %copy-start.15 = (s32[8]{0:T(128)S(1)}, s32[8]{0:T(128)}, u32[]{:S(2)}) copy-start(s32[8]{0:T(128)} %param.18) | copy-start | bytes 100
  14.7 2.1 %copy-start.10 = (bf16[3,8,2048]{2,1,0:T(8,128)(2,1)S(1)}, bf16[3,8,2048]{2,1,0:T(8,128)(2,1)}, u32[]{:S(2)}) copy-start(bf16[3,8,2048]{2,1,0:T(8,128)(2,1)} %param.12) | copy-start | bytes 294916
  16.9 42.3 %copy-start.5 = (bf16[3,8,2048]{2,1,0:T(8,128)(2,1)}, bf16[3,8,2048]{2,1,0:T(8,128)(2,1)S(1)}, u32[]{:S(2)}) copy-start(bf16[3,8,2048]{2,1,0:T(8,128)(2,1)S(1)} %add_convert_fusion) | copy-start | bytes 294916
  16.9 25.2 %collective-permute-start.6 = (bf16[24,2048]{1,0:T(8,128)(2,1)S(1)}, bf16[24,2048]{1,0:T(8,128)(2,1)S(1)}, u32[]{:S(2)}, u32[]{:S(2)}) collective-permute-start(bf16[24,2048]{1,0:T(8,128)(2,1)S(1)} %bitcast.94), channel_id=1, source_target_pairs={{0,16},{16,0},{1,17},{17,1},{2,18},{18,2},{3,19},{19,3},{4,20},{20... | collective-permute-start | bytes 294920 | tf_op jit(solution)/shard_map/ppermute | solution.py:229
  42.1 16.7 %collective-permute-start.8 = (bf16[2,24,2048]{2,1,0:T(8,128)(2,1)S(1)}, bf16[2,24,2048]{2,1,0:T(8,128)(2,1)S(1)}, u32[]{:S(2)}, u32[]{:S(2)}) collective-permute-start(bf16[2,24,2048]{2,1,0:T(8,128)(2,1)S(1)} %get-tuple-element.25), channel_id=1, source_target_pairs={{0,8},{1,9},{2,10},{3,11},{4,12},{5,13},{6,14},{7,15},{8,0},{9,1},... | collective-permute-start | bytes 589832 | tf_op jit(solution)/shard_map/ppermute | solution.py:229
  45.0 13.8 %collective-permute-start.7 = (bf16[2,24,2048]{2,1,0:T(8,128)(2,1)S(1)}, bf16[2,24,2048]{2,1,0:T(8,128)(2,1)S(1)}, u32[]{:S(2)}, u32[]{:S(2)}) collective-permute-start(bf16[2,24,2048]{2,1,0:T(8,128)(2,1)S(1)} %get-tuple-element.25), channel_id=1, source_target_pairs={{0,4},{1,5},{2,6},{3,7},{4,8},{5,9},{6,10},{7,11},{8,12},{9,13},{1... | collective-permute-start | bytes 589832 | tf_op jit(solution)/shard_map/ppermute | solution.py:229
  46.6 12.6 %collective-permute-start.9 = (bf16[2,24,2048]{2,1,0:T(8,128)(2,1)S(1)}, bf16[2,24,2048]{2,1,0:T(8,128)(2,1)S(1)}, u32[]{:S(2)}, u32[]{:S(2)}) collective-permute-start(bf16[2,24,2048]{2,1,0:T(8,128)(2,1)S(1)} %get-tuple-element.25), channel_id=1, source_target_pairs={{0,12},{1,13},{2,14},{3,15},{4,0},{5,1},{6,2},{7,3},{8,4},{9,5},{1... | collective-permute-start | bytes 589832 | tf_op jit(solution)/shard_map/ppermute | solution.py:229
  59.3 4.0 %copy-start.2 = (bf16[4,2,24,2048]{3,2,1,0:T(8,128)(2,1)}, bf16[4,2,24,2048]{3,2,1,0:T(8,128)(2,1)S(1)}, u32[]{:S(2)}) copy-start(bf16[4,2,24,2048]{3,2,1,0:T(8,128)(2,1)S(1)} %pad_maximum_fusion.4) | copy-start | bytes 2359300
  59.3 16.9 %collective-permute-start.12 = (bf16[4,2,24,2048]{3,2,1,0:T(8,128)(2,1)S(1)}, bf16[4,2,24,2048]{3,2,1,0:T(8,128)(2,1)S(1)}, u32[]{:S(2)}, u32[]{:S(2)}) collective-permute-start(bf16[4,2,24,2048]{3,2,1,0:T(8,128)(2,1)S(1)} %pad_maximum_fusion.4), channel_id=1, source_target_pairs={{0,2},{1,3},{2,0},{3,1},{4,6},{5,7},{6,4},{7,5},{8,10},{9,11},{10,... | collective-permute-start | bytes 2359304 | tf_op jit(solution)/shard_map/ppermute | solution.py:229
  63.3 16.6 %collective-permute-start.13 = (bf16[384,1024]{1,0:T(8,128)(2,1)S(1)}, bf16[384,1024]{1,0:T(8,128)(2,1)S(1)}, u32[]{:S(2)}, u32[]{:S(2)}) collective-permute-start(bf16[384,1024]{1,0:T(8,128)(2,1)S(1)} %get-tuple-element.18), channel_id=1, source_target_pairs={{0,16},{16,0},{1,17},{17,1},{2,18},{18,2},{3,19},{19,3},{4,20},{20... | collective-permute-start | bytes 2359304 | tf_op jit(solution)/shard_map/ppermute | solution.py:157
  76.2 0.9 copy-start.8
  77.1 2.7 %copy-start.11 = (f32[3,8,8]{2,1,0:T(8,128)S(1)}, f32[3,8,8]{2,1,0:T(8,128)}, u32[]{:S(2)}) copy-start(f32[3,8,8]{2,1,0:T(8,128)} %param.20) | copy-start | bytes 2308
  77.1 2.7 %copy-start.12 = (s32[3,8,8]{2,1,0:T(8,128)S(1)}, s32[3,8,8]{2,1,0:T(8,128)}, u32[]{:S(2)}) copy-start(s32[3,8,8]{2,1,0:T(8,128)} %param.19) | copy-start | bytes 2308
  79.8 22.1 %copy-start.16 = (bf16[384,1024]{1,0:T(8,128)(2,1)}, bf16[384,1024]{1,0:T(8,128)(2,1)S(1)}, u32[]{:S(2)}) copy-start(bf16[384,1024]{1,0:T(8,128)(2,1)S(1)} %collective-permute-done.13) | copy-start | bytes 2359300
  79.8 25.0 %collective-permute-start.14 = (bf16[2,4,2,24,2048]{4,3,2,1,0:T(8,128)(2,1)S(1)}, bf16[2,4,2,24,2048]{4,3,2,1,0:T(8,128)(2,1)}, u32[]{:S(2)}, u32[]{:S(2)}) collective-permute-start(bf16[2,4,2,24,2048]{4,3,2,1,0:T(8,128)(2,1)S(1)} %pad_maximum_fusion.1), channel_id=1, source_target_pairs={{0,1},{1,0},{2,3},{3,2},{4,5},{5,4},{6,7},{7,6},{8,9},{9,8},{10,11... | collective-permute-start | bytes 4718600 | tf_op jit(solution)/shard_map/ppermute | solution.py:229
  80.0 3.8 %collective-permute-start = (f32[24,16]{1,0:T(8,128)S(1)}, f32[24,16]{1,0:T(8,128)S(1)}, u32[]{:S(2)}, u32[]{:S(2)}) collective-permute-start(f32[24,16]{1,0:T(8,128)S(1)} %bitcast.102), channel_id=1, source_target_pairs={{0,16},{16,0},{1,17},{17,1},{2,18},{18,2},{3,19},{19,3},{4,20},{20... | collective-permute-start | bytes 4616 | tf_op jit(solution)/shard_map/ppermute | solution.py:229
  83.8 11.7 %collective-permute-start.2 = (f32[2,24,16]{2,1,0:T(8,128)S(1)}, f32[2,24,16]{2,1,0:T(8,128)S(1)}, u32[]{:S(2)}, u32[]{:S(2)}) collective-permute-start(f32[2,24,16]{2,1,0:T(8,128)S(1)} %get-tuple-element.31), channel_id=1, source_target_pairs={{0,8},{1,9},{2,10},{3,11},{4,12},{5,13},{6,14},{7,15},{8,0},{9,1},... | collective-permute-start | bytes 9224 | tf_op jit(solution)/shard_map/ppermute | solution.py:229
  91.6 5.6 %collective-permute-start.1 = (f32[2,24,16]{2,1,0:T(8,128)S(1)}, f32[2,24,16]{2,1,0:T(8,128)S(1)}, u32[]{:S(2)}, u32[]{:S(2)}) collective-permute-start(f32[2,24,16]{2,1,0:T(8,128)S(1)} %get-tuple-element.31), channel_id=1, source_target_pairs={{0,4},{1,5},{2,6},{3,7},{4,8},{5,9},{6,10},{7,11},{8,12},{9,13},{1... | collective-permute-start | bytes 9224 | tf_op jit(solution)/shard_map/ppermute | solution.py:229
  91.6 5.6 %collective-permute-start.3 = (f32[2,24,16]{2,1,0:T(8,128)S(1)}, f32[2,24,16]{2,1,0:T(8,128)S(1)}, u32[]{:S(2)}, u32[]{:S(2)}) collective-permute-start(f32[2,24,16]{2,1,0:T(8,128)S(1)} %get-tuple-element.31), channel_id=1, source_target_pairs={{0,12},{1,13},{2,14},{3,15},{4,0},{5,1},{6,2},{7,3},{8,4},{9,5},{1... | collective-permute-start | bytes 9224 | tf_op jit(solution)/shard_map/ppermute | solution.py:229
  97.2 4.7 %collective-permute-start.4 = (f32[4,2,24,16]{3,2,1,0:T(8,128)S(1)}, f32[4,2,24,16]{3,2,1,0:T(8,128)S(1)}, u32[]{:S(2)}, u32[]{:S(2)}) collective-permute-start(f32[4,2,24,16]{3,2,1,0:T(8,128)S(1)} %get-tuple-element.29), channel_id=1, source_target_pairs={{0,2},{1,3},{2,0},{3,1},{4,6},{5,7},{6,4},{7,5},{8,10},{9,11},{10,... | collective-permute-start | bytes 36872 | tf_op jit(solution)/shard_map/ppermute | solution.py:229
  102.0 1.6 collective-permute-start.5
  106.6 6.0 %copy-start.1 = (bf16[2,2,4,2,24,2048]{5,4,3,2,1,0:T(8,128)(2,1)}, bf16[2,2,4,2,24,2048]{5,4,3,2,1,0:T(8,128)(2,1)S(1)}, u32[]{:S(2)}) copy-start(bf16[2,2,4,2,24,2048]{5,4,3,2,1,0:T(8,128)(2,1)S(1)} %pad_maximum_fusion) | copy-start | bytes 9437188
  110.3 2.2 %copy-start.4 = (bf16[1,1024,768]{2,1,0:T(8,128)(2,1)S(1)}, bf16[1,1024,768]{2,1,0:T(8,128)(2,1)}, u32[]{:S(2)}) copy-start(bf16[1,1024,768]{2,1,0:T(8,128)(2,1)} %param.21) | copy-start | bytes 4718596
  112.6 1.1 copy-start.7
  123.1 3.5 %collective-permute-start.15 = (bf16[384,2048]{1,0:T(8,128)(2,1)S(1)}, bf16[384,2048]{1,0:T(8,128)(2,1)S(1)}, u32[]{:S(2)}, u32[]{:S(2)}) collective-permute-start(bf16[384,2048]{1,0:T(8,128)(2,1)S(1)} %slice.91), channel_id=1, source_target_pairs={{0,1},{1,0},{2,3},{3,2},{4,5},{5,4},{6,7},{7,6},{8,9},{9,8},{10,11... | collective-permute-start | bytes 4718600 | tf_op jit(solution)/shard_map/ppermute | solution.py:229
  129.1 19.7 %collective-permute-start.16 = (bf16[192,2048]{1,0:T(8,128)(2,1)S(1)}, bf16[192,2048]{1,0:T(8,128)(2,1)S(1)}, u32[]{:S(2)}, u32[]{:S(2)}) collective-permute-start(bf16[192,2048]{1,0:T(8,128)(2,1)S(1)} %slice.92), channel_id=1, source_target_pairs={{0,2},{1,3},{2,0},{3,1},{4,6},{5,7},{6,4},{7,5},{8,10},{9,11},{10,... | collective-permute-start | bytes 2359304 | tf_op jit(solution)/shard_map/ppermute | solution.py:229
  149.7 9.5 %collective-permute-start.17 = (bf16[48,2048]{1,0:T(8,128)(2,1)}, bf16[48,2048]{1,0:T(8,128)(2,1)}, u32[]{:S(2)}, u32[]{:S(2)}) collective-permute-start(bf16[48,2048]{1,0:T(8,128)(2,1)} %get-tuple-element.19), channel_id=1, source_target_pairs={{0,12},{1,13},{2,14},{3,15},{4,0},{5,1},{6,2},{7,3},{8,4},{9,5},{1... | collective-permute-start | bytes 589832 | tf_op jit(solution)/shard_map/ppermute | solution.py:229
  153.5 10.1 %collective-permute-start.19 = (bf16[48,2048]{1,0:T(8,128)(2,1)S(1)}, bf16[48,2048]{1,0:T(8,128)(2,1)}, u32[]{:S(2)}, u32[]{:S(2)}) collective-permute-start(bf16[48,2048]{1,0:T(8,128)(2,1)S(1)} %get-tuple-element.20), channel_id=1, source_target_pairs={{0,4},{1,5},{2,6},{3,7},{4,8},{5,9},{6,10},{7,11},{8,12},{9,13},{1... | collective-permute-start | bytes 589832 | tf_op jit(solution)/shard_map/ppermute | solution.py:229
  153.5 15.3 %collective-permute-start.18 = (bf16[48,2048]{1,0:T(8,128)(2,1)S(1)}, bf16[48,2048]{1,0:T(8,128)(2,1)}, u32[]{:S(2)}, u32[]{:S(2)}) collective-permute-start(bf16[48,2048]{1,0:T(8,128)(2,1)S(1)} %get-tuple-element.21), channel_id=1, source_target_pairs={{0,8},{1,9},{2,10},{3,11},{4,12},{5,13},{6,14},{7,15},{8,0},{9,1},... | collective-permute-start | bytes 589832 | tf_op jit(solution)/shard_map/ppermute | solution.py:229
  170.0 5.5 %copy-start.6 = (bf16[3,8,2048]{2,1,0:T(8,128)(2,1)S(1)}, bf16[3,8,2048]{2,1,0:T(8,128)(2,1)}, u32[]{:S(2)}) copy-start(bf16[3,8,2048]{2,1,0:T(8,128)(2,1)} %copy-done.5) | copy-start | bytes 294916
  170.8 4.7 %collective-permute-start.20 = (bf16[24,2048]{1,0:T(8,128)(2,1)S(1)}, bf16[24,2048]{1,0:T(8,128)(2,1)S(1)}, u32[]{:S(2)}, u32[]{:S(2)}) collective-permute-start(bf16[24,2048]{1,0:T(8,128)(2,1)S(1)} %fusion.40), channel_id=1, source_target_pairs={{0,16},{16,0},{1,17},{17,1},{2,18},{18,2},{3,19},{19,3},{4,20},{20... | collective-permute-start | bytes 294920 | tf_op jit(solution)/shard_map/ppermute | solution.py:229
